TPU v7x, 512 devices: a whole 4x8x8 slice. The times are simulated.
512 devices in a mesh: seq: 128 (over y, z, core), mp: 4 (over x).
Axes of the slice: x: 4, y: 8, z: 8, core: 2. Of those that a mesh axis runs over, the one named last changes fastest.
Arguments:
- layer_input: bfloat16 [16384, 2048], P('seq', 'mp'), may hold values from -6 to 6
- output_grad: bfloat16 [16384, 2048], P('seq', 'mp'), may hold values from -6 to 6
- w_out: bfloat16 [512, 2048], P('mp'), may hold values from -0.125 to 0.125
- query_heads: bfloat16 [4, 16384, 128], P('mp', 'seq'), may hold values from -32 to 32
- key_heads: bfloat16 [4, 16384, 128], P('mp', 'seq'), may hold values from -8 to 8
- value_heads: bfloat16 [4, 16384, 128], P('mp', 'seq'), may hold values from -6 to 6
- cluster_ids: int32 [4, 16384, 1], P('mp', 'seq'), may hold values from 0 to 63, as said below
Outputs:
- query_grad: bfloat16 [4, 16384, 128], P('mp', 'seq')
- key_grad: bfloat16 [4, 16384, 128], P('mp', 'seq')
- value_grad: bfloat16 [4, 16384, 128], P('mp', 'seq')
- weight_grad: float32 [2048, 1536], P('seq', 'mp')
Inputs may be any that keep to these rules, and one draw needn't show every extreme that they name: `cluster_ids`: in each head and among each index of seq's 128 tokens, every cluster holds exactly 2 tokens.
All inputs are finite; a program needn't handle non-finite values.
Results may differ from a plain program's by a relative error of at most 0.018.
Values may be sent and summed in bfloat16 or wider, within the bound.
A program may use at most 64 MiB of HBM per device.

v0:
```python
import math

import jax
import jax.numpy as jnp
from jax import lax
from jax.sharding import PartitionSpec as P

CLUSTERS = 64
MOST = 2


def attend(
    query_rows, query_place, query_live, key_rows, value_rows, grad_rows, key_live, score_scale
):
    key_place = jnp.arange(key_rows.shape[0], dtype=jnp.int32)
    causal = key_place[None, :] <= query_place[:, None]
    allowed = causal[None, :, :] & query_live.T[:, :, None] & key_live.T[:, None, :]
    scores = (
        jnp.einsum("ice,jce->cij", query_rows, key_rows, preferred_element_type=jnp.float32)
        * score_scale
    )
    scores = jnp.where(allowed, scores, -1e30)
    row_max = jnp.max(scores, axis=2, keepdims=True)
    weights = jnp.exp(scores - row_max)
    probs = jnp.where(allowed, weights / jnp.sum(weights, axis=2, keepdims=True), 0.0)
    probs_low = probs.astype(jnp.bfloat16)
    attended = jnp.einsum("cij,jce->ice", probs_low, value_rows, preferred_element_type=jnp.float32)
    row_delta = jnp.sum(grad_rows.astype(jnp.float32) * attended, axis=2)
    prob_grad = jnp.einsum(
        "ice,jce->cij", grad_rows, value_rows, preferred_element_type=jnp.float32
    )
    dscore = (probs * (prob_grad - row_delta.T[:, :, None])).astype(jnp.bfloat16)
    query_part = (
        jnp.einsum("cij,jce->ice", dscore, key_rows, preferred_element_type=jnp.float32)
        * score_scale
    )
    key_part = (
        jnp.einsum("cij,ice->jce", dscore, query_rows, preferred_element_type=jnp.float32)
        * score_scale
    )
    value_part = jnp.einsum(
        "cij,ice->jce", probs_low, grad_rows, preferred_element_type=jnp.float32
    )
    return (query_part, key_part, value_part)


def on_device(layer_input, output_grad, w_out, query_heads, key_heads, value_heads, cluster_ids):
    seq_count = lax.axis_size("seq")
    head_dim = query_heads.shape[2]
    capacity = MOST
    copies = max(1, seq_count // CLUSTERS)
    per_owner = max(1, CLUSTERS // seq_count)
    groups = CLUSTERS // per_owner
    slot_count = seq_count * capacity
    score_scale = 1.0 / math.sqrt(head_dim)
    members = cluster_ids[0, :, 0]
    onehot = (members[:, None] == jnp.arange(CLUSTERS, dtype=jnp.int32)[None, :]).astype(jnp.int32)
    before = jnp.cumsum(onehot, axis=0) - onehot
    slot = jnp.sum(before * onehot, axis=1)
    counts = jnp.sum(onehot, axis=0)
    target = (members // per_owner * capacity + slot) * per_owner + members % per_owner
    tally_send = jnp.broadcast_to(
        counts.reshape(groups, 1, per_owner), (groups, copies, per_owner)
    ).reshape(seq_count, per_owner)
    tallies = lax.all_to_all(tally_send, "seq", split_axis=0, concat_axis=0, tiled=True)
    inputs_full, grad_full = (
        lax.all_gather(layer_input, "mp", axis=1, tiled=True),
        lax.all_gather(output_grad, "mp", axis=1, tiled=True),
    )
    head_grad = lax.dot_general(
        grad_full, w_out, (((1,), (1,)), ((), ())), preferred_element_type=jnp.float32
    ).astype(jnp.bfloat16)
    packed = jnp.concatenate([query_heads[0], key_heads[0], value_heads[0], head_grad], axis=1)
    width = packed.shape[1]
    buffer = jnp.zeros((groups * capacity * per_owner, width), packed.dtype).at[target].set(packed)
    buffer = jnp.broadcast_to(
        buffer.reshape(groups, 1, capacity * per_owner * width),
        (groups, copies, capacity * per_owner * width),
    )
    received = lax.all_to_all(
        buffer.reshape(slot_count, per_owner, width), "seq", split_axis=0, concat_axis=0, tiled=True
    )
    query_rows = received[:, :, 0:head_dim]
    key_rows = received[:, :, head_dim : 2 * head_dim]
    value_rows = received[:, :, 2 * head_dim : 3 * head_dim]
    grad_rows = received[:, :, 3 * head_dim : 4 * head_dim]
    slot_place = jnp.arange(slot_count, dtype=jnp.int32)
    source = slot_place // capacity
    slot_live = (slot_place % capacity)[:, None] < jnp.repeat(tallies, capacity, axis=0)
    own_copy = lax.axis_index("seq") % copies
    query_live = slot_live & (source % copies == own_copy)[:, None]
    query_full, key_part, value_part = attend(
        query_rows, slot_place, query_live, key_rows, value_rows, grad_rows, slot_live, score_scale
    )
    stacked = jnp.concatenate([query_full, key_part, value_part], axis=2)
    returned = lax.all_to_all(
        stacked.astype(jnp.bfloat16), "seq", split_axis=0, concat_axis=0, tiled=True
    ).astype(stacked.dtype)
    summed = jnp.sum(returned.reshape(groups, copies, capacity * per_owner, 3 * head_dim), axis=1)
    token_grads = summed.reshape(groups * capacity * per_owner, 3 * head_dim)[target]
    low_grads = token_grads.astype(jnp.bfloat16)
    weight_grad = lax.psum_scatter(
        lax.dot_general(
            inputs_full, low_grads, (((0,), (0,)), ((), ())), preferred_element_type=jnp.float32
        ),
        "seq",
        scatter_dimension=0,
        tiled=True,
    )
    query_grad = low_grads[:, 0:head_dim][None]
    key_grad = low_grads[:, head_dim : 2 * head_dim][None]
    value_grad = low_grads[:, 2 * head_dim : 3 * head_dim][None]
    return (query_grad, key_grad, value_grad, weight_grad)


def solution(mesh):
    return jax.shard_map(
        on_device,
        mesh=mesh,
        in_specs=(
            P("seq", "mp"),
            P("seq", "mp"),
            P("mp", None),
            P("mp", "seq", None),
            P("mp", "seq", None),
            P("mp", "seq", None),
            P("mp", "seq", None),
        ),
        out_specs=(
            P("mp", "seq", None),
            P("mp", "seq", None),
            P("mp", "seq", None),
            P("seq", "mp"),
        ),
        check_vma=False,
    )
```

profile of v0, /device:TPU:1, one launch (start us, length us, event | category | flops | bytes accessed | tf_op | source)
XLA Modules:
  0.0 315.4 jit_solution(11110220609439896026)
XLA Ops:
  7.2 0.0 copy-start
  7.2 0.8 fusion.17
  8.0 0.2 reduce_window_sum.11
  8.2 0.8 fusion.20
  9.0 0.1 broadcast_in_dim.51
  9.1 0.7 broadcast_in_dim.60
  9.8 18.4 %all-to-all-start.1 = ((s32[128,1,1]{2,1,0:T(1,128)}), s32[128,1,1]{2,1,0:T(1,128)S(1)}, u32[]{:S(2)}, u32[]{:S(2)}) async-start(s32[128,1,1]{2,1,0:T(1,128)} %broadcast_in_dim.60), calls=%async_computation.1 | async-start | bytes 131072 | tf_op jit(solution)/shard_map/all_to_all | solution.py:65
  28.2 0.9 copy.34
  29.1 0.9 copy.35
  30.0 0.9 copy.36
  30.8 0.7 fusion.24
  31.5 11.9 %all_gather.6 = bf16[128,2048]{1,0:T(8,128)(2,1)S(1)} all-gather(bf16[128,512]{1,0:T(8,128)(2,1)} %param.8), channel_id=1, replica_groups=mesh['seq'=128,'mp'=4] {'mp'}, dimensions={1}, use_global_device_ids=true | all-gather | bytes 655360 | tf_op jit(solution)/shard_map/all_gather | solution.py:68
  43.4 0.0 copy-done
  43.4 0.3 convolution_convert_fusion.1
  43.7 0.1 copy.37
  43.8 1.1 scatter_custom_fusion
  45.0 0.1 broadcast_in_dim.50
  45.1 0.2 reshape.265
  45.4 0.5 broadcast.231
  45.9 2.2 reduce.8
  48.1 0.8 reshape.273
  48.9 0.0 all-to-all-done.1
  48.9 15.2 %all-to-all-start = ((bf16[128,2,512]{2,1,0:T(2,128)(2,1)}), bf16[128,2,512]{2,1,0:T(2,128)(2,1)S(1)}, u32[]{:S(2)}, u32[]{:S(2)}) async-start(bf16[128,2,512]{2,1,0:T(2,128)(2,1)} %reshape.273), calls=%async_computation | async-start | bytes 524288 | tf_op jit(solution)/shard_map/all_to_all | solution.py:80
  64.1 2.4 reduce.5
  66.5 0.1 broadcast_in_dim.53
  66.5 0.2 broadcast_in_dim.54
  66.7 11.6 %all-to-all-done = bf16[128,2,512]{2,1,0:T(2,128)(2,1)S(1)} async-done(((bf16[128,2,512]{2,1,0:T(2,128)(2,1)}), bf16[128,2,512]{2,1,0:T(2,128)(2,1)S(1)}, u32[]{:S(2)}, u32[]{:S(2)}) %all-to-all-start) | async-done | bytes 262176 | tf_op jit(solution)/shard_map/all_to_all | solution.py:80
  78.3 0.2 reshape.274
  78.6 0.5 fusion.26
  79.1 0.1 copy.54
  79.2 0.2 fusion.27
  79.5 0.1 fusion.12
  79.5 0.0 copy-start.1
  79.5 0.3 fusion.7
  79.8 0.3 fusion.6
  80.1 0.2 fusion.2
  80.3 0.2 fusion.8
  80.5 0.2 fusion.9
  80.7 0.8 reduce.9
  81.5 0.2 copy.70
  81.6 0.8 reshape.275
  82.4 7.1 %all-to-all-start.2 = ((bf16[128,2,384]{2,1,0:T(2,128)(2,1)}), bf16[128,2,384]{2,1,0:T(2,128)(2,1)S(1)}, u32[]{:S(2)}, u32[]{:S(2)}) async-start(bf16[128,2,384]{2,1,0:T(2,128)(2,1)} %reshape.275), calls=%async_computation.2 | async-start | bytes 393216 | tf_op jit(solution)/shard_map/all_to_all | solution.py:96
  89.5 0.0 reduce-scatter.4.cloned.1.call-start
  89.6 0.0 copy-done.1
  89.6 11.7 %all_gather.7 = bf16[128,2048]{1,0:T(8,128)(2,1)S(1)} all-gather(bf16[128,512]{1,0:T(8,128)(2,1)S(1)} %copy-done.1), channel_id=1, replica_groups=mesh['seq'=128,'mp'=4] {'mp'}, dimensions={1}, use_global_device_ids=true | all-gather | bytes 655360 | tf_op jit(solution)/shard_map/all_gather | solution.py:67
  101.3 1.5 all-to-all-done.2
  102.8 0.1 reshape.276
  102.9 1.1 convert_reduce_fusion
  104.0 0.2 reshape.248
  104.3 0.3 reduce_sum.52
  104.7 0.9 gather_fusion
  105.5 2.3 convolution_bitcast_fusion
  107.8 3.6 %copy.48 = f32[2048,384]{1,0:T(8,128)} copy(f32[2048,384]{0,1:T(8,128)} %convolution_bitcast_fusion) | data formatting | bytes 6291456
  111.4 0.0 reduce-scatter.4.cloned.1.call-update
  111.4 0.6 slice_bitcast_fusion
  112.0 196.5 %reduce-scatter.4.cloned.1.call-done = f32[16,384]{1,0:T(8,128)} async-done(((f32[2048,384]{1,0:T(8,128)}), f32[16,384]{1,0:T(8,128)}) %reduce-scatter.4.cloned.1.call-update) | async-done | bytes 24592
  (6 shorter events, 0.1 us)
Async XLA Ops:
  7.2 36.2 %copy-start = (bf16[128,2048]{1,0:T(8,128)(2,1)S(1)}, bf16[128,2048]{1,0:T(8,128)(2,1)}, u32[]{:S(2)}) copy-start(bf16[128,2048]{1,0:T(8,128)(2,1)} %param.9) | copy-start | bytes 1572868
  9.8 39.1 %all-to-all-start.1 = ((s32[128,1,1]{2,1,0:T(1,128)}), s32[128,1,1]{2,1,0:T(1,128)S(1)}, u32[]{:S(2)}, u32[]{:S(2)}) async-start(s32[128,1,1]{2,1,0:T(1,128)} %broadcast_in_dim.60), calls=%async_computation.1 | async-start | bytes 131072 | tf_op jit(solution)/shard_map/all_to_all | solution.py:65
  48.9 29.4 %all-to-all-start = ((bf16[128,2,512]{2,1,0:T(2,128)(2,1)}), bf16[128,2,512]{2,1,0:T(2,128)(2,1)S(1)}, u32[]{:S(2)}, u32[]{:S(2)}) async-start(bf16[128,2,512]{2,1,0:T(2,128)(2,1)} %reshape.273), calls=%async_computation | async-start | bytes 524288 | tf_op jit(solution)/shard_map/all_to_all | solution.py:80
  79.5 10.1 %copy-start.1 = (bf16[128,512]{1,0:T(8,128)(2,1)S(1)}, bf16[128,512]{1,0:T(8,128)(2,1)}, u32[]{:S(2)}) copy-start(bf16[128,512]{1,0:T(8,128)(2,1)} %param.7) | copy-start | bytes 393220
  82.4 20.4 %all-to-all-start.2 = ((bf16[128,2,384]{2,1,0:T(2,128)(2,1)}), bf16[128,2,384]{2,1,0:T(2,128)(2,1)S(1)}, u32[]{:S(2)}, u32[]{:S(2)}) async-start(bf16[128,2,384]{2,1,0:T(2,128)(2,1)} %reshape.275), calls=%async_computation.2 | async-start | bytes 393216 | tf_op jit(solution)/shard_map/all_to_all | solution.py:96
  89.5 219.0 %reduce-scatter.4.cloned.1.call-start = ((), (), s32[]{:S(2)}) async-start(), calls=%async_computation.4 | async-start | bytes 3170304
Sparse Core Ops, SparseCore 0:
  111.5 196.9 reduce-scatter.3
where the time goes:
time: 320 us; the launch traced here: 315 us
  waiting for transfers between devices  210 us (66%)
  starting transfers between devices  40.8 us (13%)
  blocking collectives  23.6 us (7%)
  between operations  14.3 us (4%)
  local copies, waits for them, and re-layouts  13.9 us (4%)
  other arithmetic  9.31 us (3%)
  matrix products  3.9 us (1%)
    unnamed x2, waiting for transfers between devices  197 us
    all_to_all x1, starting transfers between devices, on_device(): lax.all_to_all(tally_send, 'seq', split_axis=0, concat_axis=0, tiled=True)  18.4 us
    all_to_all x1, starting transfers between devices, on_device(): lax.all_to_all(buffer.reshape(slot_count, per_owner, width), 'seq', split...  15.2 us
    all_gather x1, blocking collectives, on_device(): lax.all_gather(output_grad, 'mp', axis=1, tiled=True)  11.9 us
    all_gather x1, blocking collectives, on_device(): lax.all_gather(layer_input, 'mp', axis=1, tiled=True)  11.7 us
    all_to_all x1, waiting for transfers between devices, on_device(): lax.all_to_all(buffer.reshape(slot_count, per_owner, width), 'seq', split...  11.6 us
    unnamed x14, local copies, waits for them, and re-layouts  8.38 us
    all_to_all x1, starting transfers between devices, on_device(): lax.all_to_all(stacked.astype(jnp.bfloat16), 'seq', split_axis=0, concat_...  7.13 us
  transfers between devices with their start and end apart: 4, of which 3 were waited for; matrix products, arithmetic and copies ran while one was open for 4% of the time, Pallas kernels for 0%

commit v1 on v0

v1 whole, which is shorter than its diff:
```python
import math

import jax
import jax.numpy as jnp
from jax import lax
from jax.experimental import pallas as pl
from jax.experimental.pallas import tpu as pltpu
from jax.sharding import PartitionSpec as P

MOST = 2
KINDS = 4
MESSAGE = MOST * KINDS
FEATS = 16
MESH = pl.DeviceIdType.MESH
F32 = jnp.float32
BF16 = jnp.bfloat16
NT = (((1,), (1,)), ((), ()))
TN = (((0,), (0,)), ((), ()))


def dot(left, right, dims=(((1,), (0,)), ((), ()))):
    return lax.dot_general(left, right, dims, preferred_element_type=F32)


def iota(shape, dim):
    return lax.broadcasted_iota(jnp.int32, shape, dim)


def as_bf16(mask):
    return jnp.where(mask, 1.0, 0.0).astype(BF16)


def copy_to(src, dst, send_sem, recv_sem, device):
    return pltpu.make_async_remote_copy(
        src_ref=src,
        dst_ref=dst,
        send_sem=send_sem,
        recv_sem=recv_sem,
        device_id=device,
        device_id_type=MESH,
    )


def kernel(
    side,
    heads,
    grad_ref,
    input_ref,
    w_ref,
    q_ref,
    k_ref,
    v_ref,
    cid_ref,
    dq_ref,
    dk_ref,
    dv_ref,
    wg_ref,
    grad_land,
    input_land,
    pick,
    unpick,
    packed,
    send1,
    land1,
    land2,
    back1,
    land3,
    land4,
    turned,
    turned_land,
    low_grads,
    part_send,
    part_land,
    part_sum,
    last_land,
    x_send,
    x_recv,
    i_send,
    i_recv,
    s1_send,
    s1_recv,
    s2_send,
    s2_recv,
    b1_send,
    b1_recv,
    b2_send,
    b2_recv,
    t_send,
    t_recv,
    g_send,
    g_recv,
    p_send,
    p_recv,
    l_send,
    l_recv,
):
    n = side
    shift = n.bit_length() - 1
    tokens = grad_ref.shape[0]
    cols = grad_ref.shape[1]
    head_dim = w_ref.shape[0]
    clusters = n * n
    rows = clusters * MESSAGE
    scale = 1.0 / math.sqrt(head_dim)

    seq = lax.axis_index("seq")
    mp = lax.axis_index("mp")
    core = seq % 2
    y = seq // 2 // n
    z = seq // 2 % n
    a = y + core * (z - y)
    b = z + core * (y - z)

    def device(first, second, which):
        py = first + which * (second - first)
        pz = second + which * (first - second)
        return ((py * n + pz) * 2 + which, mp)

    def loop(low, high, body):
        def step(i, carry):
            body(i)
            return carry

        lax.fori_loop(low, high, step, 0)

    barrier = pltpu.get_barrier_semaphore()

    def greet(to):
        pl.semaphore_signal(barrier, inc=1, device_id=to, device_id_type=MESH)

    def greet_lines(i):
        there_y = (y + i) % n
        there_z = (z + i) % n
        for which in range(2):
            greet(((there_y * n + z) * 2 + which, mp))
            greet(((y * n + there_z) * 2 + which, mp))

    loop(1, n, greet_lines)
    greet((seq + 1 - 2 * core, mp))
    for off in range(1, heads):
        greet((seq, (mp + off) % heads))

    cid = cid_ref[0]
    along = jnp.broadcast_to(cid, (tokens, tokens))
    at_row = iota((tokens, tokens), 0)
    at_col = iota((tokens, tokens), 1)
    cid_row = jnp.sum(jnp.where(at_row == at_col, along, 0), axis=0, keepdims=True)
    same = along == cid_row
    slot_row = jnp.sum(jnp.where(same & (at_row < at_col), 1, 0), axis=0, keepdims=True)
    slot_col = jnp.sum(jnp.where(same & (at_col < at_row), 1, 0), axis=1, keepdims=True)
    step_a = n - core * (n - 1)
    step_b = 1 + core * (n - 1)

    def token_key(r):
        group = lax.shift_right_logical(r, 3)
        first = lax.shift_right_logical(group, shift)
        second = group & (n - 1)
        return (first * step_a + second * step_b) * 2 + (r & 1)

    target_row = cid_row * 2 + slot_row
    target_col = cid * 2 + slot_col
    r_col = iota((rows, 1), 0)
    r_row = iota((1, rows), 1)
    key_col = token_key(r_col)
    key_row = token_key(r_row)
    kind_col = lax.shift_right_logical(r_col, 1) & 3
    kind_row = lax.shift_right_logical(r_row, 1) & 3
    total = None
    for kind, ref in enumerate((q_ref, k_ref, v_ref)):
        chosen = as_bf16(jnp.where(kind_col == kind, key_col, -1) == target_row)
        term = dot(chosen, ref[0])
        total = term if total is None else total + term
        unpick[kind] = as_bf16(jnp.where(kind_row == kind, key_row, -1) == target_col)
    packed[...] = total
    pick[...] = as_bf16(jnp.where(kind_col == 3, key_col, -1) == target_row)

    partners = (2 * n - 1) + 2 * (n - 1) + heads - 1
    pl.semaphore_wait(barrier, partners)

    def x_copy(src, land, sends, recvs, off):
        return copy_to(
            src, land.at[off - 1], sends.at[off - 1], recvs.at[off - 1], (seq, (mp + off) % heads)
        )

    for off in range(1, heads):
        x_copy(grad_ref, grad_land, x_send, x_recv, off).start()

    def w_part(owner):
        return w_ref[:, pl.ds(pl.multiple_of(owner * cols, cols), cols)]

    head_grad = dot(grad_ref[...], w_part(mp), NT)
    for off in range(1, heads):
        x_copy(grad_ref, grad_land, x_send, x_recv, off).wait_recv()
        head_grad += dot(grad_land[off - 1], w_part((mp + heads - off) % heads), NT)
    for off in range(1, heads):
        x_copy(input_ref, input_land, i_send, i_recv, off).start()
    filled = packed[...] + dot(pick[...], head_grad.astype(BF16))
    send1[...] = filled.reshape(clusters, MESSAGE, head_dim).astype(BF16)

    def first_copy(off, to, source):
        return copy_to(
            send1.at[pl.ds(to * n, n)],
            land1.at[source],
            s1_send.at[off],
            s1_recv.at[off],
            device(to, b, core),
        )

    loop(1, n, lambda i: first_copy(i, (a + i) % n, a).start())
    land1[a] = send1[pl.ds(a * n, n)]
    loop(1, n, lambda i: first_copy(i, a, (a + n - i) % n).wait_recv())

    def second_copy(off, to, which, source):
        return copy_to(
            land1.at[:, to],
            land2.at[which, source],
            s2_send.at[off],
            s2_recv.at[which, off],
            ((lambda d: (d[0] - which, mp))(device(a, to, which))),
        )

    @pl.when(core == 0)
    def _():
        loop(1, n, lambda i: second_copy(i, (b + i) % n, 0, b).start())
        land2[0, b] = land1[:, b]

    @pl.when(core == 1)
    def _():
        loop(0, n, lambda i: second_copy(i, (b + i) % n, 1, b).start())

    count = 2 * clusters * MOST
    lot = min(256, 2 * rows)
    part = lot // KINDS
    lots = 2 * rows // lot

    def place(p):
        which = p // (2 * clusters)
        second = p // (2 * n) % n
        first = p // 2 % n
        py = first + which * (second - first)
        pz = second + which * (first - second)
        return ((py * n + pz) * 2 + which) * 2 + p % 2

    def back_copy(off, to, which, source):
        relay = (y * n + to) * 2 if which == 0 else (to * n + z) * 2 + 1
        return copy_to(
            back1.at[which, to],
            land3.at[source],
            b1_send.at[which, off],
            b1_recv.at[off],
            (relay, mp),
        )

    @pl.when(core == 0)
    def _():
        out_row = iota((lot, lot), 0)
        in_row = iota((lot, lot), 1)
        out_at = out_row % part
        wanted = (out_at // 2) * MESSAGE + (out_row // part) * 2 + out_at % 2
        split = as_bf16(wanted == in_row)
        out_row = iota((lot, 3 * part), 0)
        in_row = iota((lot, 3 * part), 1)
        wanted = (out_row // 2 % 4) * part + (out_row // MESSAGE) * 2 + out_row % 2
        join = as_bf16(wanted == in_row)
        allowed = place(iota((count, 1), 0)) <= place(iota((1, count), 1))

        loop(1, n, lambda i: second_copy(i, b, 0, (b + n - i) % n).wait_recv())
        loop(
            0,
            n,
            lambda i: copy_to(
                land1.at[:, 0],
                land2.at[1, (y + n - i) % n],
                s2_send.at[0],
                s2_recv.at[1, i],
                (seq + 1, mp),
            ).wait_recv(),
        )
        got = land2[...].astype(F32).reshape(2 * rows, head_dim).astype(BF16)
        pieces = [[] for _ in range(KINDS)]
        for i in range(lots):
            parted = dot(split, got[i * lot : (i + 1) * lot]).astype(BF16)
            for kind in range(KINDS):
                pieces[kind].append(parted[kind * part : (kind + 1) * part])
        queries, keys, values, grads = (jnp.concatenate(p, axis=0) for p in pieces)
        scores = jnp.where(allowed, dot(keys, queries, NT) * scale, -1e30)
        weights = jnp.exp(scores - jnp.max(scores, axis=0, keepdims=True))
        probs = weights / jnp.sum(weights, axis=0, keepdims=True)
        probs_low = probs.astype(BF16)
        prob_grad = dot(values, grads, NT)
        delta = jnp.sum(probs_low.astype(F32) * prob_grad, axis=0, keepdims=True)
        dscore = (probs * (prob_grad - delta)).astype(BF16)
        value_part = dot(probs_low, grads).astype(BF16)
        key_part = (dot(dscore, queries) * scale).astype(BF16)
        query_part = (dot(dscore, keys, TN) * scale).astype(BF16)
        per = lot // MESSAGE
        outs = []
        for i in range(lots):
            span = slice(i * part, (i + 1) * part)
            three = jnp.concatenate([query_part[span], key_part[span], value_part[span]], axis=0)
            outs.append(dot(join, three))
        whole = jnp.concatenate(outs, axis=0)
        back1[...] = whole.reshape(2, n, n, MESSAGE, head_dim).astype(BF16)
        loop(1, n, lambda i: back_copy(i, (z + i) % n, 0, z).start())
        loop(0, n, lambda i: back_copy(i, (y + i) % n, 1, y).start())
        land3[b] = back1[0, b]
        loop(1, n, lambda i: back_copy(i, z, 0, (z + n - i) % n).wait_recv())

    @pl.when(core == 1)
    def _():
        loop(
            0,
            n,
            lambda i: copy_to(
                back1.at[1, 0],
                land3.at[(b + n - i) % n],
                b1_send.at[1, 0],
                b1_recv.at[i],
                (seq - 1, mp),
            ).wait_recv(),
        )

    def home_copy(off, to, source):
        return copy_to(
            land3.at[:, to],
            land4.at[source],
            b2_send.at[off],
            b2_recv.at[off],
            device(to, b, core),
        )

    loop(1, n, lambda i: home_copy(i, (a + i) % n, a).start())
    land4[a] = land3[:, a]

    for off in range(1, heads):
        x_copy(input_ref, input_land, i_send, i_recv, off).wait_recv()
    wide = 2 * FEATS * n
    out_row = iota((wide, wide), 0)
    in_row = iota((wide, wide), 1)
    half = wide // 2
    out_at = out_row % half
    wanted = (out_at // FEATS) * 2 * FEATS + (out_row // half) * FEATS + out_at % FEATS
    order = as_bf16(wanted == in_row)
    per_block = cols // wide

    def turn(block, index):
        for i in range(per_block):
            py = index * per_block + i
            done = dot(order, block[:, i * wide : (i + 1) * wide], NT).astype(BF16)
            turned[0, py] = done[0:half].reshape(n, FEATS, tokens)
            turned[1, :, py] = done[half:].reshape(n, FEATS, tokens)

    turn(input_ref[...], mp)
    for off in range(1, heads):
        turn(input_land[off - 1], (mp + heads - off) % heads)
    other = seq + 1 - 2 * core
    turn_copy = copy_to(
        turned.at[1 - core], turned_land, t_send.at[0], t_recv.at[0], (other, mp)
    )
    turn_copy.start()

    loop(1, n, lambda i: home_copy(i, a, (a + n - i) % n).wait_recv())
    home = land4[...].astype(F32).reshape(rows, head_dim).astype(BF16)
    for kind, ref in enumerate((dq_ref, dk_ref, dv_ref)):
        value = dot(unpick[kind], home).astype(BF16)
        ref[0] = value
        low_grads[core, :, kind * head_dim : (kind + 1) * head_dim] = value
    share = copy_to(
        low_grads.at[core], low_grads.at[core], g_send.at[0], g_recv.at[0], (other, mp)
    )
    share.start()
    turn_copy.wait_recv()
    copy_to(
        low_grads.at[core], low_grads.at[1 - core], g_send.at[0], g_recv.at[0], (other, mp)
    ).wait_recv()

    both = jnp.concatenate([low_grads[core], low_grads[1 - core]], axis=0)

    def partial(to):
        mine = turned[core, to].reshape(half, tokens)
        theirs = turned_land[to].reshape(half, tokens)
        return dot(jnp.concatenate([mine, theirs], axis=1), both)

    def part_copy(off, to, source):
        return copy_to(
            part_send.at[to],
            part_land.at[source],
            p_send.at[off],
            p_recv.at[off],
            device(to, b, core),
        )

    def send_part(i):
        off = (i + n // 2 - 1) % (n - 1) + 1
        to = (a + off) % n
        part_send[to] = partial(to).astype(BF16)
        part_copy(off, to, a).start()

    loop(0, n - 1, send_part)
    part_sum[...] = partial(a).reshape(part_sum.shape)

    def add_part(i):
        source = (a + n - i) % n
        part_copy(i, a, source).wait_recv()
        part_sum[...] += part_land[source].astype(F32).reshape(part_sum.shape)

    loop(1, n, add_part)

    def last_copy(off, to, source):
        return copy_to(
            part_sum.at[to], last_land.at[source], l_send.at[off], l_recv.at[off], device(a, to, core)
        )

    loop(1, n, lambda i: last_copy(i, (b + i) % n, b).start())
    wg_ref[...] = part_sum[b]

    def add_last(i):
        source = (b + n - i) % n
        last_copy(i, b, source).wait_recv()
        wg_ref[...] += last_land[source]

    loop(1, n, add_last)

    for off in range(1, heads):
        x_copy(grad_ref, grad_land, x_send, x_recv, off).wait_send()
        x_copy(input_ref, input_land, i_send, i_recv, off).wait_send()
    turn_copy.wait_send()
    share.wait_send()

    def all_sent(i):
        first_copy(i, (a + i) % n, a).wait_send()
        home_copy(i, (a + i) % n, a).wait_send()
        part_copy(i, (a + i) % n, a).wait_send()
        last_copy(i, (b + i) % n, b).wait_send()

    loop(1, n, all_sent)

    @pl.when(core == 0)
    def _():
        loop(1, n, lambda i: second_copy(i, (b + i) % n, 0, b).wait_send())
        loop(1, n, lambda i: back_copy(i, (z + i) % n, 0, z).wait_send())
        loop(0, n, lambda i: back_copy(i, (y + i) % n, 1, y).wait_send())

    @pl.when(core == 1)
    def _():
        loop(0, n, lambda i: second_copy(i, (b + i) % n, 1, b).wait_send())


def on_device(layer_input, output_grad, w_out, query_heads, key_heads, value_heads, cluster_ids):
    devices = lax.axis_size("seq")
    heads = lax.axis_size("mp")
    n = math.isqrt(devices // 2)
    tokens, cols = layer_input.shape
    head_dim = query_heads.shape[2]
    clusters = n * n
    rows = clusters * MESSAGE
    half = FEATS * n
    width = 3 * head_dim
    vmem = pl.BlockSpec(memory_space=pltpu.VMEM)
    dma = pltpu.SemaphoreType.DMA
    grad_shape = jax.ShapeDtypeStruct((1, tokens, head_dim), BF16)
    return pl.pallas_call(
        lambda *refs: kernel(n, heads, *refs),
        out_shape=(
            grad_shape,
            grad_shape,
            grad_shape,
            jax.ShapeDtypeStruct((FEATS, width), F32),
        ),
        in_specs=[vmem] * 7,
        out_specs=(vmem,) * 4,
        scratch_shapes=[
            pltpu.VMEM((heads - 1, tokens, cols), BF16),
            pltpu.VMEM((heads - 1, tokens, cols), BF16),
            pltpu.VMEM((rows, tokens), BF16),
            pltpu.VMEM((3, tokens, rows), BF16),
            pltpu.VMEM((rows, head_dim), F32),
            pltpu.VMEM((clusters, MESSAGE, head_dim), BF16),
            pltpu.VMEM((n, n, MESSAGE, head_dim), BF16),
            pltpu.VMEM((2, n, n, MESSAGE, head_dim), BF16),
            pltpu.VMEM((2, n, n, MESSAGE, head_dim), BF16),
            pltpu.VMEM((n, n, MESSAGE, head_dim), BF16),
            pltpu.VMEM((n, n, MESSAGE, head_dim), BF16),
            pltpu.VMEM((2, n, n, FEATS, tokens), BF16),
            pltpu.VMEM((n, n, FEATS, tokens), BF16),
            pltpu.VMEM((2, tokens, width), BF16),
            pltpu.VMEM((n, half, width), BF16),
            pltpu.VMEM((n, half, width), BF16),
            pltpu.VMEM((n, FEATS, width), F32),
            pltpu.VMEM((n, FEATS, width), F32),
            dma((heads - 1,)),
            dma((heads - 1,)),
            dma((heads - 1,)),
            dma((heads - 1,)),
            dma((n,)),
            dma((n,)),
            dma((n,)),
            dma((2, n)),
            dma((2, n)),
            dma((n,)),
            dma((n,)),
            dma((n,)),
            dma((1,)),
            dma((1,)),
            dma((1,)),
            dma((1,)),
            dma((n,)),
            dma((n,)),
            dma((n,)),
            dma((n,)),
        ],
        compiler_params=pltpu.CompilerParams(
            collective_id=0, has_side_effects=True, vmem_limit_bytes=32 * 1024 * 1024
        ),
    )(output_grad, layer_input, w_out, query_heads, key_heads, value_heads, cluster_ids)


def solution(mesh):
    return jax.shard_map(
        on_device,
        mesh=mesh,
        in_specs=(
            P("seq", "mp"),
            P("seq", "mp"),
            P("mp", None),
            P("mp", "seq", None),
            P("mp", "seq", None),
            P("mp", "seq", None),
            P("mp", "seq", None),
        ),
        out_specs=(
            P("mp", "seq", None),
            P("mp", "seq", None),
            P("mp", "seq", None),
            P("seq", "mp"),
        ),
        check_vma=False,
    )
```

time: 320 us -> 74.8 us (0.23); the launches traced: 315 us -> 74.5 us
  waiting for transfers between devices: 210 us -> 0 us
  Pallas kernels: 0 us -> 67 us
  starting transfers between devices: 40.8 us -> 0 us
  blocking collectives: 23.6 us -> 0 us
  between operations: 14.3 us -> 0.68 us
  other arithmetic: 9.31 us -> 0 us
  local copies, waits for them, and re-layouts: 13.9 us -> 6.84 us
  matrix products: 3.9 us -> 0 us
    unnamed x2 -> x0, waiting for transfers between devices: 197 us -> none
    pallas_call x0 -> x1, Pallas kernels: none -> 67 us  [on_device(): pl.pallas_call(lambda *refs: kernel(n, heads, *refs), out_shape=(grad_sha...]
    all_to_all x3 -> x0, starting transfers between devices: 40.8 us -> none  [the longest x1 18.4 us: on_device(): lax.all_to_all(tally_send, 'seq', split_axis=0, concat_axis=0, tiled=True)]
    all_gather x2 -> x0, blocking collectives: 23.6 us -> none  [the longest x1 11.9 us: on_device(): lax.all_gather(output_grad, 'mp', axis=1, tiled=True)]
    all_to_all x3 -> x0, waiting for transfers between devices: 13.1 us -> none  [the longest x1 11.6 us: on_device(): lax.all_to_all(buffer.reshape(slot_count, per_owner, width), 'seq', split...]
    dot_general x8 -> x0, matrix products: 3.9 us -> none  [the longest x1 2.26 us: on_device(): lax.dot_general(inputs_full, low_grads, (((0,), (0,)), ((), ())), preferr...]
    reshape x2 -> x0, other arithmetic: 3.31 us -> none  [the longest x1 2.21 us: on_device(): buffer.reshape(slot_count, per_owner, width)]
    unnamed x14 -> x17, local copies, waits for them, and re-layouts: 8.38 us -> 6.84 us
  transfers between devices with their start and end apart: 4 -> 0, of which waited for: 3 -> 0; matrix products, arithmetic and copies ran while one was open for 4% -> 0% of each run, Pallas kernels for 0% -> 0%
where the time goes in v1:
time: 74.8 us; the launch traced here: 74.5 us
  Pallas kernels  67 us (90%)
  local copies, waits for them, and re-layouts  6.84 us (9%)
    pallas_call x1, Pallas kernels, on_device(): pl.pallas_call(lambda *refs: kernel(n, heads, *refs), out_shape=(grad_sha...  67 us
    unnamed x17, local copies, waits for them, and re-layouts  6.84 us

profile of v1, /device:TPU:1, one launch (start us, length us, event | category | flops | bytes accessed | tf_op | source)
XLA Modules:
  0.0 74.5 jit_solution(10053904205434348969)
XLA Ops:
  0.6 0.0 copy-start.4
  0.6 0.0 copy-start.3
  0.7 0.8 %copy.11.refs_6_ = s32[1,128,1]{2,1,0:T(8,128)S(1)} copy(s32[1,128,1]{1,2,0:T(1,128)} %param.13) | data formatting | bytes 1024 | tf_op args[6]
  1.4 0.0 copy-done.4
  1.4 0.0 copy-done.3
  1.4 0.0 copy-start
  1.5 1.0 %copy-done = bf16[128,2048]{1,0:T(8,128)(2,1)S(1)} copy-done((bf16[128,2048]{1,0:T(8,128)(2,1)S(1)}, bf16[128,2048]{1,0:T(8,128)(2,1)}, u32[]{:S(2)}) %copy-start) | copy-done | bytes 524312
  2.5 0.0 copy-start.1
  2.5 0.9 %copy-done.1 = bf16[128,512]{1,0:T(8,128)(2,1)S(1)} copy-done((bf16[128,512]{1,0:T(8,128)(2,1)S(1)}, bf16[128,512]{1,0:T(8,128)(2,1)}, u32[]{:S(2)}) %copy-start.1) | copy-done | bytes 131096
  3.4 0.0 copy-start.2
  3.4 0.9 %copy-done.2 = bf16[128,512]{1,0:T(8,128)(2,1)S(1)} copy-done((bf16[128,512]{1,0:T(8,128)(2,1)S(1)}, bf16[128,512]{1,0:T(8,128)(2,1)}, u32[]{:S(2)}) %copy-start.2) | copy-done | bytes 131096
  4.3 0.0 copy-start.5
  4.3 0.8 %copy-done.5 = bf16[1,128,128]{2,1,0:T(8,128)(2,1)S(1)} copy-done((bf16[1,128,128]{2,1,0:T(8,128)(2,1)S(1)}, bf16[1,128,128]{2,1,0:T(8,128)(2,1)}, u32[]{:S(2)}) %copy-start.5) | copy-done | bytes 32792
  5.1 67.0 %shard_map.102 = (bf16[1,128,128]{2,1,0:T(8,128)(2,1)S(1)}, bf16[1,128,128]{2,1,0:T(8,128)(2,1)S(1)}, bf16[1,128,128]{2,1,0:T(8,128)(2,1)S(1)}, f32[16,384]{1,0:T(8,128)S(1)}) custom-call(bf16[128,512]{1,0:T(8,128)(2,1)S(1)} %copy-done.1, bf16[128,512]{1,0:T(8,128)(2,1)S(1)} %copy-done.2, bf16[128,2048]{1,0:T(8,128)(2,1)S(1)} %copy-done, ...), custom_call_target="tpu_custom_call" | custom-call | tf_op jit(solution)/shard_map/pallas_call | solution.py:462
  72.0 0.6 copy.16
  72.6 0.6 copy.17
  73.2 0.6 copy.18
  73.9 0.6 copy.19
Async XLA Ops:
  0.6 0.8 %copy-start.4 = (bf16[1,128,128]{2,1,0:T(8,128)(2,1)S(1)}, bf16[1,128,128]{2,1,0:T(8,128)(2,1)}, u32[]{:S(2)}) copy-start(bf16[1,128,128]{2,1,0:T(8,128)(2,1)} %refs_4_.1) | copy-start | bytes 98308
  0.6 0.8 %copy-start.3 = (bf16[1,128,128]{2,1,0:T(8,128)(2,1)S(1)}, bf16[1,128,128]{2,1,0:T(8,128)(2,1)}, u32[]{:S(2)}) copy-start(bf16[1,128,128]{2,1,0:T(8,128)(2,1)} %refs_3_.1) | copy-start | bytes 98308
  1.4 1.0 %copy-start = (bf16[128,2048]{1,0:T(8,128)(2,1)S(1)}, bf16[128,2048]{1,0:T(8,128)(2,1)}, u32[]{:S(2)}) copy-start(bf16[128,2048]{1,0:T(8,128)(2,1)} %refs_2_.1) | copy-start | bytes 1572868
  2.5 0.9 %copy-start.1 = (bf16[128,512]{1,0:T(8,128)(2,1)S(1)}, bf16[128,512]{1,0:T(8,128)(2,1)}, u32[]{:S(2)}) copy-start(bf16[128,512]{1,0:T(8,128)(2,1)} %refs_0_.1) | copy-start | bytes 393220
  3.4 0.9 %copy-start.2 = (bf16[128,512]{1,0:T(8,128)(2,1)S(1)}, bf16[128,512]{1,0:T(8,128)(2,1)}, u32[]{:S(2)}) copy-start(bf16[128,512]{1,0:T(8,128)(2,1)} %refs_1_.1) | copy-start | bytes 393220
  4.3 0.8 %copy-start.5 = (bf16[1,128,128]{2,1,0:T(8,128)(2,1)S(1)}, bf16[1,128,128]{2,1,0:T(8,128)(2,1)}, u32[]{:S(2)}) copy-start(bf16[1,128,128]{2,1,0:T(8,128)(2,1)} %refs_5_.1) | copy-start | bytes 98308

commit v2 on v1

v2 whole, which is shorter than its diff:
```python
import math

import jax
import jax.numpy as jnp
from jax import lax
from jax.experimental import pallas as pl
from jax.experimental.pallas import tpu as pltpu
from jax.sharding import PartitionSpec as P

MOST = 2
KINDS = 4
MESSAGE = MOST * KINDS
FEATS = 16
MESH = pl.DeviceIdType.MESH
F32 = jnp.float32
BF16 = jnp.bfloat16
NT = (((1,), (1,)), ((), ()))
TN = (((0,), (0,)), ((), ()))


def dot(left, right, dims=(((1,), (0,)), ((), ()))):
    return lax.dot_general(left, right, dims, preferred_element_type=F32)


def iota(shape, dim):
    return lax.broadcasted_iota(jnp.int32, shape, dim)


def as_bf16(mask):
    return jnp.where(mask, 1.0, 0.0).astype(BF16)


def copy_to(src, dst, send_sem, recv_sem, device):
    return pltpu.make_async_remote_copy(
        src_ref=src,
        dst_ref=dst,
        send_sem=send_sem,
        recv_sem=recv_sem,
        device_id=device,
        device_id_type=MESH,
    )


def loop(low, high, body):
    def step(i, carry):
        body(i)
        return carry

    lax.fori_loop(low, high, step, 0)


def take(ref, sem):
    pltpu.make_async_copy(ref, ref, sem).wait()


def slots(cid_row):
    tokens = cid_row.shape[1]
    across = jnp.broadcast_to(cid_row, (tokens, tokens))
    at_row = iota((tokens, tokens), 0)
    at_col = iota((tokens, tokens), 1)
    cid_col = jnp.sum(jnp.where(at_row == at_col, across, 0), axis=1, keepdims=True)
    same = across == cid_col
    slot_row = jnp.sum(jnp.where(same & (at_row < at_col), 1, 0), axis=0, keepdims=True)
    slot_col = jnp.sum(jnp.where(same & (at_col < at_row), 1, 0), axis=1, keepdims=True)
    return slot_row, cid_col, slot_col


def kernel(
    side,
    heads,
    grad_hbm,
    input_hbm,
    w_hbm,
    q_hbm,
    k_hbm,
    v_hbm,
    cid_hbm,
    grads_out,
    wg_out,
    grad_ref,
    input_ref,
    w_ref,
    qkv_ref,
    cid_ref,
    in_sem,
    out_sem,
    ready,
    grad_land,
    pick,
    unpick,
    packed,
    send1,
    land2,
    back1,
    home,
    piece0,
    piece1,
    turned,
    low_grads,
    part_send,
    part_land,
    part_sum,
    last_land,
    wg_ref,
    c_send,
    c_recv,
    x_send,
    x_recv,
    i_send,
    i_recv,
    s_send,
    s_recv,
    b_send,
    b_recv,
    h_send,
    h_recv,
    p_send,
    p_recv,
    l_send,
    l_recv,
):
    n = side
    tokens, cols = grad_ref.shape
    head_dim = w_ref.shape[0]
    clusters = n * n
    rows = clusters * MESSAGE
    scale = 1.0 / math.sqrt(head_dim)
    seq = lax.axis_index("seq")
    mp = lax.axis_index("mp")
    core = lax.rem(seq, 2)
    chip = seq // 2
    y = chip // n
    z = lax.rem(chip, n)
    other = seq + 1 - 2 * core
    a = y + core * (z - y)
    b = z + core * (y - z)

    def device(first, second):
        py = first + core * (second - first)
        pz = second + core * (first - second)
        return ((py * n + pz) * 2 + core, mp)

    def far_first(i):
        block = i // (clusters // 4)
        at = lax.rem(i, clusters // 4)

        def far(k):
            return lax.rem(n // 2 + n + (1 - 2 * lax.rem(k, 2)) * ((k + 1) // 2), n)

        dy = far(at // (n // 2) + (n // 2) * (block // 2))
        dz = far(lax.rem(at, n // 2) + (n // 2) * lax.rem(block, 2))
        return lax.rem(y + dy, n) * n + lax.rem(z + dz, n)

    sent = []

    barrier = pltpu.get_barrier_semaphore()

    def greet(to):
        pl.semaphore_signal(barrier, inc=1, device_id=to, device_id_type=MESH)

    def greet_lines(i):
        there_y = lax.rem(y + i, n)
        there_z = lax.rem(z + i, n)
        greet(((there_y * n + z) * 2 + core, mp))
        greet(((y * n + there_z) * 2 + core, mp))
        greet(((y * n + there_z) * 2 + 1 - core, mp))

    for off in range(1, heads):
        greet((seq, lax.rem(mp + off, heads)))
        greet((other, lax.rem(mp + off, heads)))
    greet((other, mp))
    loop(1, n, greet_lines)
    fetches = [
        pltpu.make_async_copy(src, dst, in_sem.at[i])
        for i, (src, dst) in enumerate(
            (
                (grad_hbm, grad_ref),
                (w_hbm, w_ref),
                (cid_hbm, cid_ref.at[core]),
                (q_hbm, qkv_ref.at[pl.ds(0, 1)]),
                (k_hbm, qkv_ref.at[pl.ds(1, 1)]),
                (v_hbm, qkv_ref.at[pl.ds(2, 1)]),
                (input_hbm, input_ref),
            )
        )
    ]
    for fetch in fetches:
        fetch.start()
    pl.semaphore_wait(barrier, 3 * (n - 1) + 1 + 2 * (heads - 1))

    def grad_copy(off):
        return copy_to(
            grad_hbm,
            grad_land.at[off - 1],
            x_send.at[off - 1],
            x_recv.at[off - 1],
            (seq, lax.rem(mp + off, heads)),
        )

    for off in range(1, heads):
        grad_copy(off).start()
        sent.append(grad_copy(off).wait_send)
    loop(
        1,
        n,
        lambda i: pl.semaphore_signal(
            ready,
            inc=1,
            device_id=((lax.rem(y + i, n) * n + z) * 2 + core, mp),
            device_id_type=MESH,
        ),
    )
    fetches[2].wait()
    cid_copy = copy_to(
        cid_ref.at[core], cid_ref.at[core], c_send.at[0], c_recv.at[0], (other, mp)
    )
    cid_copy.start()
    sent.append(cid_copy.wait_send)

    cid_row = cid_ref[core]
    slot_row = slots(cid_row)[0]
    target_row = cid_row * MOST + slot_row
    r_col = iota((rows, 1), 0)
    key_col = (r_col // MESSAGE) * MOST + r_col % MOST
    kind_col = r_col // MOST % KINDS
    for i in range(3, 6):
        fetches[i].wait()
    total = None
    for kind in range(3):
        chosen = as_bf16(jnp.where(kind_col == kind, key_col, -1) == target_row)
        term = dot(chosen, qkv_ref[kind])
        total = term if total is None else total + term
    packed[...] = total
    pick[...] = as_bf16(jnp.where(kind_col == 3, key_col, -1) == target_row)

    fetches[6].wait()
    wide = 2 * FEATS * n
    half = wide // 2
    out_row = iota((wide, wide), 0)
    in_row = iota((wide, wide), 1)
    out_at = out_row % half
    wanted = (out_at // FEATS) * 2 * FEATS + (out_row // half) * FEATS + out_at % FEATS
    order = as_bf16(wanted == in_row)
    blocks = cols // wide
    for i in range(blocks):
        done = dot(order, input_ref[:, i * wide : (i + 1) * wide], NT).astype(BF16)
        piece0[i] = done[0:half].reshape(n, FEATS, tokens)
        piece1[:, i] = done[half:].reshape(n, FEATS, tokens)

    take(cid_ref.at[0], c_recv.at[0])
    home_rows = 2 * rows
    r_row = iota((1, home_rows), 1)
    spot = r_row // (2 * MESSAGE)
    which = spot // (clusters // 2)
    from_cluster = (spot - which * (clusters // 2)) * 2 + which
    key_row = (from_cluster * 2 + r_row // MESSAGE % 2) * MOST + r_row % MOST
    kind_row = r_row // MOST % KINDS
    for of in range(2):
        _, cid_col, slot_col = slots(cid_ref[of])
        wanted = (cid_col * 2 + of) * MOST + slot_col
        for kind in range(3):
            at = (of * 3 + kind) * tokens
            unpick[at : at + tokens] = as_bf16(
                jnp.where(kind_row == kind, key_row, -1) == wanted
            )

    def w_part(owner):
        return w_ref[:, pl.ds(pl.multiple_of(owner * cols, cols), cols)]

    fetches[0].wait()
    fetches[1].wait()
    head_grad = dot(grad_ref[...], w_part(mp), NT)
    for off in range(1, heads):
        grad_copy(off).wait_recv()
        head_grad += dot(grad_land[off - 1], w_part(lax.rem(mp + heads - off, heads)), NT)
    filled = packed[...] + dot(pick[...], head_grad.astype(BF16))
    send1[...] = filled.reshape(clusters, MESSAGE, head_dim).astype(BF16)
    pl.semaphore_wait(ready, n - 1)

    def to_owner(i):
        to = far_first(i)
        copy_to(
            send1.at[to], land2.at[seq], s_send.at[0], s_recv.at[0], (to * 2, mp)
        ).start()

    loop(0, clusters - 1 + core, to_owner)

    @pl.when(core == 0)
    def _():
        land2[seq] = send1[chip]

    def owner_sent():
        @pl.when(core == 0)
        def _():
            take(send1.at[pl.ds(0, clusters - 1)], s_send.at[0])

        @pl.when(core == 1)
        def _():
            take(send1, s_send.at[0])

    sent.append(owner_sent)

    def input_copy(off, of, to, received=False):
        at = pl.ds(lax.rem(mp + heads - off, heads) * blocks, blocks)
        here = pl.ds(mp * blocks, blocks)
        src, mine, theirs = (
            (piece0, turned.at[of, here], turned.at[of, at])
            if to == 0
            else (piece1, turned.at[of, :, here], turned.at[of, :, at])
        )
        sems = (i_send.at[2 * off + to], i_recv.at[2 * off + of])
        goal = (seq - core + to, lax.rem(mp + off, heads))
        return copy_to(src, theirs if received else mine, *sems, goal)

    def inputs(act):
        for off in range(heads):
            for to in range(2):
                if off == 0:

                    @pl.when(core != to)
                    def _():
                        act(off, to)
                else:
                    act(off, to)

    inputs(lambda off, to: input_copy(off, core, to).start())
    sent.append(lambda: inputs(lambda off, to: input_copy(off, core, to).wait_send()))

    @pl.when(core == 0)
    def _():
        turned[0, pl.ds(mp * blocks, blocks)] = piece0[...]

    @pl.when(core == 1)
    def _():
        turned[1, :, pl.ds(mp * blocks, blocks)] = piece1[...]

    @pl.when(core == 0)
    def _():
        take(land2.at[pl.ds(0, 2 * clusters - 1)], s_recv.at[0])

    count = 2 * clusters * MOST
    lot = min(256, 2 * rows)
    part = lot // KINDS
    lots = 2 * rows // lot

    def to_home(i, to_core):
        to = far_first(i)
        copy_to(
            back1.at[to],
            home.at[to_core, chip // 2],
            b_send.at[0],
            b_recv.at[0],
            (to * 2 + to_core, mp),
        ).start()

    even = lax.rem(chip, 2) == 0

    @pl.when(core == 0)
    def _():
        out_row = iota((lot, lot), 0)
        in_row = iota((lot, lot), 1)
        out_at = out_row % part
        wanted = (out_at // 2) * MESSAGE + (out_row // part) * 2 + out_at % 2
        split = as_bf16(wanted == in_row)
        out_row = iota((lot, 3 * part), 0)
        in_row = iota((lot, 3 * part), 1)
        wanted = (out_row // 2 % 4) * part + (out_row // MESSAGE) * 2 + out_row % 2
        join = as_bf16(wanted == in_row)
        allowed = iota((count, count), 0) <= iota((count, count), 1)
        got = land2[...].astype(F32).reshape(2 * rows, head_dim).astype(BF16)
        pieces = [[] for _ in range(KINDS)]
        for i in range(lots):
            parted = dot(split, got[i * lot : (i + 1) * lot]).astype(BF16)
            for kind in range(KINDS):
                pieces[kind].append(parted[kind * part : (kind + 1) * part])
        queries, keys, values, grads = (jnp.concatenate(p, axis=0) for p in pieces)
        scores = jnp.where(allowed, dot(keys, queries, NT) * scale, -1e30)
        weights = jnp.exp(scores - jnp.max(scores, axis=0, keepdims=True))
        probs = weights / jnp.sum(weights, axis=0, keepdims=True)
        probs_low = probs.astype(BF16)
        prob_grad = dot(values, grads, NT)
        delta = jnp.sum(probs_low.astype(F32) * prob_grad, axis=0, keepdims=True)
        dscore = (probs * (prob_grad - delta)).astype(BF16)
        value_part = dot(probs_low, grads).astype(BF16)
        key_part = (dot(dscore, queries) * scale).astype(BF16)
        query_part = (dot(dscore, keys, TN) * scale).astype(BF16)
        outs = []
        for i in range(lots):
            span = slice(i * part, (i + 1) * part)
            three = jnp.concatenate([query_part[span], key_part[span], value_part[span]], axis=0)
            outs.append(dot(join, three))
        whole = jnp.concatenate(outs, axis=0).astype(BF16)
        back1[...] = whole.reshape(clusters, 2 * MESSAGE, head_dim)

        @pl.when(even)
        def _():
            loop(0, clusters - 1, lambda i: to_home(i, 0))
            home[0, chip // 2] = back1[chip]

        @pl.when(jnp.logical_not(even))
        def _():
            loop(0, clusters, lambda i: to_home(i, 1))

    def back_sent():
        @pl.when((core == 0) & even)
        def _():
            take(back1.at[pl.ds(0, clusters - 1)], b_send.at[0])

        @pl.when((core == 0) & jnp.logical_not(even))
        def _():
            take(back1, b_send.at[0])

    sent.append(back_sent)

    @pl.when((core == 0) & even)
    def _():
        take(home.at[0, pl.ds(0, clusters // 2 - 1)], b_recv.at[0])

    @pl.when((core == 1) | jnp.logical_not(even))
    def _():
        take(home.at[0], b_recv.at[0])

    swap = copy_to(home.at[core], home.at[core], h_send.at[0], h_recv.at[0], (other, mp))
    swap.start()
    sent.append(swap.wait_send)
    take(home.at[0], h_recv.at[0])

    ordered = dot(unpick[...], home[...].reshape(home_rows, head_dim)).astype(BF16)
    for of in range(2):
        for kind in range(3):
            at = (of * 3 + kind) * tokens
            low_grads[of, :, kind * head_dim : (kind + 1) * head_dim] = ordered[at : at + tokens]
    out_copies = [
        pltpu.make_async_copy(
            low_grads.at[core, :, pl.ds(kind * head_dim, head_dim)],
            grads_out.at[kind],
            out_sem.at[kind],
        )
        for kind in range(3)
    ]
    for out_copy in out_copies:
        out_copy.start()
        sent.append(out_copy.wait)
    for mine in range(2):

        @pl.when(core == mine)
        def _():
            for off in range(heads):
                for of in range(2):
                    if off or of != mine:
                        input_copy(off, of, mine, True).wait_recv()

    both = jnp.concatenate([low_grads[0], low_grads[1]], axis=0)

    def partial(to):
        left = [turned[of, to].reshape(half, tokens) for of in range(2)]
        return dot(jnp.concatenate(left, axis=1), both)

    def part_copy(off, to, source):
        return copy_to(
            part_send.at[to], part_land.at[source], p_send.at[off], p_recv.at[off], device(to, b)
        )

    def send_part(i):
        off = lax.rem(i + n // 2 - 1, n - 1) + 1
        to = lax.rem(a + off, n)
        part_send[to] = partial(to).astype(BF16)
        part_copy(off, to, a).start()

    loop(0, n - 1, send_part)
    sent.append(lambda: loop(1, n, lambda i: part_copy(i, lax.rem(a + i, n), a).wait_send()))
    part_sum[...] = partial(a).reshape(part_sum.shape)

    def add_part(i):
        source = lax.rem(a + n - i, n)
        part_copy(i, a, source).wait_recv()
        part_sum[...] += part_land[source].astype(F32).reshape(part_sum.shape)

    loop(1, n, add_part)

    def last_copy(off, to, source):
        return copy_to(
            part_sum.at[to], last_land.at[source], l_send.at[off], l_recv.at[off], device(a, to)
        )

    loop(1, n, lambda i: last_copy(i, lax.rem(b + i, n), b).start())
    sent.append(lambda: loop(1, n, lambda i: last_copy(i, lax.rem(b + i, n), b).wait_send()))
    wg_ref[...] = part_sum[b]

    def add_last(i):
        source = lax.rem(b + n - i, n)
        last_copy(i, b, source).wait_recv()
        wg_ref[...] += last_land[source]

    loop(1, n, add_last)
    wg_copy = pltpu.make_async_copy(wg_ref, wg_out, out_sem.at[3])
    wg_copy.start()
    sent.append(wg_copy.wait)

    for wait_sent in sent:
        wait_sent()


def hand_out(grads_in, wg_in, dq_out, dk_out, dv_out, wg_out):
    for kind, out in enumerate((dq_out, dk_out, dv_out)):
        out[0] = grads_in[kind]
    wg_out[...] = wg_in[...]


def on_device(layer_input, output_grad, w_out, query_heads, key_heads, value_heads, cluster_ids):
    devices = lax.axis_size("seq")
    heads = lax.axis_size("mp")
    n = math.isqrt(devices // 2)
    tokens, cols = layer_input.shape
    head_dim = query_heads.shape[2]
    clusters = n * n
    rows = clusters * MESSAGE
    half = FEATS * n
    blocks = cols // (2 * half)
    width = 3 * head_dim
    hbm = pl.BlockSpec(memory_space=pltpu.HBM)
    dma = pltpu.SemaphoreType.DMA
    grad_shape = jax.ShapeDtypeStruct((1, tokens, head_dim), BF16)
    wg_shape = jax.ShapeDtypeStruct((FEATS, width), F32)
    grads, weight_grad = pl.pallas_call(
        lambda *refs: kernel(n, heads, *refs),
        out_shape=(jax.ShapeDtypeStruct((3, tokens, head_dim), BF16), wg_shape),
        in_specs=[hbm] * 7,
        out_specs=(hbm, hbm),
        scratch_shapes=[
            pltpu.VMEM((tokens, cols), BF16),
            pltpu.VMEM((tokens, cols), BF16),
            pltpu.VMEM((head_dim, heads * cols), BF16),
            pltpu.VMEM((3, tokens, head_dim), BF16),
            pltpu.VMEM((2, 1, tokens), jnp.int32),
            dma((7,)),
            dma((4,)),
            pltpu.SemaphoreType.REGULAR,
            pltpu.VMEM((heads - 1, tokens, cols), BF16),
            pltpu.VMEM((rows, tokens), BF16),
            pltpu.VMEM((6 * tokens, 2 * rows), BF16),
            pltpu.VMEM((rows, head_dim), F32),
            pltpu.VMEM((clusters, MESSAGE, head_dim), BF16),
            pltpu.VMEM((2 * clusters, MESSAGE, head_dim), BF16),
            pltpu.VMEM((clusters, 2 * MESSAGE, head_dim), BF16),
            pltpu.VMEM((2, clusters // 2, 2 * MESSAGE, head_dim), BF16),
            pltpu.VMEM((blocks, n, FEATS, tokens), BF16),
            pltpu.VMEM((n, blocks, FEATS, tokens), BF16),
            pltpu.VMEM((2, n, n, FEATS, tokens), BF16),
            pltpu.VMEM((2, tokens, width), BF16),
            pltpu.VMEM((n, half, width), BF16),
            pltpu.VMEM((n, half, width), BF16),
            pltpu.VMEM((n, FEATS, width), F32),
            pltpu.VMEM((n, FEATS, width), F32),
            pltpu.VMEM((FEATS, width), F32),
            dma((1,)),
            dma((1,)),
            dma((heads - 1,)),
            dma((heads - 1,)),
            dma((2 * heads,)),
            dma((2 * heads,)),
            dma((1,)),
            dma((1,)),
            dma((1,)),
            dma((1,)),
            dma((1,)),
            dma((1,)),
            dma((n,)),
            dma((n,)),
            dma((n,)),
            dma((n,)),
        ],
        compiler_params=pltpu.CompilerParams(
            collective_id=0, has_side_effects=True, vmem_limit_bytes=64 * 1024 * 1024
        ),
    )(
        output_grad,
        layer_input,
        w_out,
        query_heads,
        key_heads,
        value_heads,
        cluster_ids.reshape(1, tokens),
    )
    return pl.pallas_call(
        hand_out,
        out_shape=(grad_shape, grad_shape, grad_shape, wg_shape),
        in_specs=[pl.BlockSpec(memory_space=pltpu.VMEM)] * 2,
        out_specs=(pl.BlockSpec(memory_space=pltpu.VMEM),) * 4,
        compiler_params=pltpu.CompilerParams(vmem_limit_bytes=64 * 1024 * 1024),
    )(grads, weight_grad)


def solution(mesh):
    return jax.shard_map(
        on_device,
        mesh=mesh,
        in_specs=(
            P("seq", "mp"),
            P("seq", "mp"),
            P("mp", None),
            P("mp", "seq", None),
            P("mp", "seq", None),
            P("mp", "seq", None),
            P("mp", "seq", None),
        ),
        out_specs=(
            P("mp", "seq", None),
            P("mp", "seq", None),
            P("mp", "seq", None),
            P("seq", "mp"),
        ),
        check_vma=False,
    )
```

time: 74.8 us -> 63.5 us (0.85)
  local copies, waits for them, and re-layouts: 6.84 us -> 0 us
  Pallas kernels: 67 us -> 62.7 us
    unnamed x17 -> x0, local copies, waits for them, and re-layouts: 6.84 us -> none
    pallas_call x1 -> x2, Pallas kernels: 67 us -> 62.7 us  [the longest x1 61.2 us: on_device(): pl.pallas_call(lambda *refs: kernel(n, heads, *refs), out_shape=(jax.Shap...]
where the time goes in v2:
time: 63.5 us; the launch traced here: 63.4 us
  Pallas kernels  62.7 us (99%)
  between operations  0.64 us (1%)
    pallas_call x1, Pallas kernels, on_device(): pl.pallas_call(lambda *refs: kernel(n, heads, *refs), out_shape=(jax.Shap...  61.2 us
    pallas_call x1, Pallas kernels, on_device(): pl.pallas_call(hand_out, out_shape=(grad_shape, grad_shape, grad_shape, w...  1.54 us

profile of v2, /device:TPU:1, one launch (start us, length us, event | category | flops | bytes accessed | tf_op | source)
XLA Modules:
  0.0 63.4 jit_solution(16708321150234376272)
XLA Ops:
  0.6 61.2 %shard_map.102 = (bf16[3,128,128]{2,1,0:T(8,128)(2,1)}, f32[16,384]{1,0:T(8,128)}) custom-call(bf16[128,512]{1,0:T(8,128)(2,1)} %refs_0_.1, bf16[128,512]{1,0:T(8,128)(2,1)} %refs_1_.1, bf16[128,2048]{1,0:T(8,128)(2,1)} %refs_2_.1, bf16[1,128,128]{2,1,0:T(8,128)(2,1)} %refs_3_.1, bf16[1,128,128]{2,1,0:T(8,128)(2,1)} %refs_4_.1, ...), custom_call_target="tpu_custom_call" | custom-call | tf_op jit(solution)/shard_map/pallas_call | solution.py:525
  61.8 1.5 %shard_map.103 = (bf16[1,128,128]{2,1,0:T(8,128)(2,1)}, bf16[1,128,128]{2,1,0:T(8,128)(2,1)}, bf16[1,128,128]{2,1,0:T(8,128)(2,1)}, f32[16,384]{1,0:T(8,128)}) custom-call(bf16[3,128,128]{2,1,0:T(8,128)(2,1)} %get-tuple-element.6.grads_in, f32[16,384]{1,0:T(8,128)} %get-tuple-element.7.wg_in), custom_call_target="tpu_custom_call" | custom-call | tf_op jit(solution)/shard_map/pallas_call | solution.py:585

commit v3 on v2

--- a/solution.py
+++ b/solution.py
@@ -39,14 +39,6 @@
         device_id=device,
         device_id_type=MESH,
     )
-
-
-def loop(low, high, body):
-    def step(i, carry):
-        body(i)
-        return carry
-
-    lax.fori_loop(low, high, step, 0)
 
 
 def take(ref, sem):
@@ -100,6 +92,7 @@
     part_send,
     part_land,
     part_sum,
+    last_send,
     last_land,
     wg_ref,
     c_send,
@@ -140,16 +133,14 @@
         pz = second + core * (first - second)
         return ((py * n + pz) * 2 + core, mp)
 
-    def far_first(i):
-        block = i // (clusters // 4)
-        at = lax.rem(i, clusters // 4)
-
-        def far(k):
-            return lax.rem(n // 2 + n + (1 - 2 * lax.rem(k, 2)) * ((k + 1) // 2), n)
-
-        dy = far(at // (n // 2) + (n // 2) * (block // 2))
-        dz = far(lax.rem(at, n // 2) + (n // 2) * lax.rem(block, 2))
-        return lax.rem(y + dy, n) * n + lax.rem(z + dz, n)
+    ys = [lax.rem(y + d, n) for d in range(n)]
+    zs = [lax.rem(z + d, n) for d in range(n)]
+    firsts = [ys[d] + core * (zs[d] - ys[d]) for d in range(n)]
+    seconds = [zs[d] + core * (ys[d] - zs[d]) for d in range(n)]
+    away = sorted(
+        ((dy, dz) for dy in range(n) for dz in range(n) if dy or dz),
+        key=lambda d: -min(d[0], n - d[0]) - min(d[1], n - d[1]),
+    )
 
     sent = []
 
@@ -157,19 +148,15 @@
 
     def greet(to):
         pl.semaphore_signal(barrier, inc=1, device_id=to, device_id_type=MESH)
-
-    def greet_lines(i):
-        there_y = lax.rem(y + i, n)
-        there_z = lax.rem(z + i, n)
-        greet(((there_y * n + z) * 2 + core, mp))
-        greet(((y * n + there_z) * 2 + core, mp))
-        greet(((y * n + there_z) * 2 + 1 - core, mp))
 
     for off in range(1, heads):
         greet((seq, lax.rem(mp + off, heads)))
         greet((other, lax.rem(mp + off, heads)))
     greet((other, mp))
-    loop(1, n, greet_lines)
+    for d in range(1, n):
+        greet(((ys[d] * n + z) * 2 + core, mp))
+        greet(((y * n + zs[d]) * 2 + core, mp))
+        greet(((y * n + zs[d]) * 2 + 1 - core, mp))
     fetches = [
         pltpu.make_async_copy(src, dst, in_sem.at[i])
         for i, (src, dst) in enumerate(
@@ -190,26 +177,21 @@
 
     def grad_copy(off):
         return copy_to(
-            grad_hbm,
+            grad_ref,
             grad_land.at[off - 1],
             x_send.at[off - 1],
             x_recv.at[off - 1],
             (seq, lax.rem(mp + off, heads)),
         )
 
+    fetches[0].wait()
     for off in range(1, heads):
         grad_copy(off).start()
         sent.append(grad_copy(off).wait_send)
-    loop(
-        1,
-        n,
-        lambda i: pl.semaphore_signal(
-            ready,
-            inc=1,
-            device_id=((lax.rem(y + i, n) * n + z) * 2 + core, mp),
-            device_id_type=MESH,
-        ),
-    )
+    for d in range(1, n):
+        pl.semaphore_signal(
+            ready, inc=1, device_id=((ys[d] * n + z) * 2 + core, mp), device_id_type=MESH
+        )
     fetches[2].wait()
     cid_copy = copy_to(
         cid_ref.at[core], cid_ref.at[core], c_send.at[0], c_recv.at[0], (other, mp)
@@ -233,6 +215,45 @@
     packed[...] = total
     pick[...] = as_bf16(jnp.where(kind_col == 3, key_col, -1) == target_row)
 
+    def w_part(owner):
+        return w_ref[:, pl.ds(pl.multiple_of(owner * cols, cols), cols)]
+
+    fetches[1].wait()
+    head_grad = dot(grad_ref[...], w_part(mp), NT)
+    for off in range(1, heads):
+        grad_copy(off).wait_recv()
+        head_grad += dot(grad_land[off - 1], w_part(lax.rem(mp + heads - off, heads)), NT)
+    filled = packed[...] + dot(pick[...], head_grad.astype(BF16))
+    send1[...] = filled.reshape(clusters, MESSAGE, head_dim).astype(BF16)
+    pl.semaphore_wait(ready, n - 1)
+
+    def to_owner(to):
+        copy_to(
+            send1.at[to], land2.at[seq], s_send.at[0], s_recv.at[0], (to * 2, mp)
+        ).start()
+
+    for dy, dz in away:
+        to_owner(ys[dy] * n + zs[dz])
+
+    @pl.when(core == 0)
+    def _():
+        land2[seq] = send1[chip]
+
+    @pl.when(core == 1)
+    def _():
+        to_owner(chip)
+
+    def owner_sent():
+        @pl.when(core == 0)
+        def _():
+            take(send1.at[pl.ds(0, clusters - 1)], s_send.at[0])
+
+        @pl.when(core == 1)
+        def _():
+            take(send1, s_send.at[0])
+
+    sent.append(owner_sent)
+
     fetches[6].wait()
     wide = 2 * FEATS * n
     half = wide // 2
@@ -248,57 +269,18 @@
         piece1[:, i] = done[half:].reshape(n, FEATS, tokens)
 
     take(cid_ref.at[0], c_recv.at[0])
-    home_rows = 2 * rows
-    r_row = iota((1, home_rows), 1)
-    spot = r_row // (2 * MESSAGE)
-    which = spot // (clusters // 2)
-    from_cluster = (spot - which * (clusters // 2)) * 2 + which
-    key_row = (from_cluster * 2 + r_row // MESSAGE % 2) * MOST + r_row % MOST
+    r_row = iota((1, rows), 1)
+    key_row = (r_row // (2 * MESSAGE) * 4 + r_row // MESSAGE % 2) * MOST + r_row % MOST
     kind_row = r_row // MOST % KINDS
     for of in range(2):
         _, cid_col, slot_col = slots(cid_ref[of])
         wanted = (cid_col * 2 + of) * MOST + slot_col
         for kind in range(3):
             at = (of * 3 + kind) * tokens
-            unpick[at : at + tokens] = as_bf16(
-                jnp.where(kind_row == kind, key_row, -1) == wanted
-            )
-
-    def w_part(owner):
-        return w_ref[:, pl.ds(pl.multiple_of(owner * cols, cols), cols)]
-
-    fetches[0].wait()
-    fetches[1].wait()
-    head_grad = dot(grad_ref[...], w_part(mp), NT)
-    for off in range(1, heads):
-        grad_copy(off).wait_recv()
-        head_grad += dot(grad_land[off - 1], w_part(lax.rem(mp + heads - off, heads)), NT)
-    filled = packed[...] + dot(pick[...], head_grad.astype(BF16))
-    send1[...] = filled.reshape(clusters, MESSAGE, head_dim).astype(BF16)
-    pl.semaphore_wait(ready, n - 1)
-
-    def to_owner(i):
-        to = far_first(i)
-        copy_to(
-            send1.at[to], land2.at[seq], s_send.at[0], s_recv.at[0], (to * 2, mp)
-        ).start()
-
-    loop(0, clusters - 1 + core, to_owner)
-
-    @pl.when(core == 0)
-    def _():
-        land2[seq] = send1[chip]
-
-    def owner_sent():
-        @pl.when(core == 0)
-        def _():
-            take(send1.at[pl.ds(0, clusters - 1)], s_send.at[0])
-
-        @pl.when(core == 1)
-        def _():
-            take(send1, s_send.at[0])
-
-    sent.append(owner_sent)
+            for odd in range(2):
+                unpick[odd, at : at + tokens] = as_bf16(
+                    jnp.where(kind_row == kind, key_row + 2 * MOST * odd, -1) == wanted
+                )
 
     def input_copy(off, of, to, received=False):
         at = pl.ds(lax.rem(mp + heads - off, heads) * blocks, blocks)
@@ -343,17 +325,17 @@
     part = lot // KINDS
     lots = 2 * rows // lot
 
-    def to_home(i, to_core):
-        to = far_first(i)
+    odd = lax.rem(chip, 2)
+    even = odd == 0
+
+    def to_home(to):
         copy_to(
             back1.at[to],
-            home.at[to_core, chip // 2],
+            home.at[odd, chip // 2],
             b_send.at[0],
             b_recv.at[0],
-            (to * 2 + to_core, mp),
+            (to * 2 + odd, mp),
         ).start()
-
-    even = lax.rem(chip, 2) == 0
 
     @pl.when(core == 0)
     def _():
@@ -392,14 +374,16 @@
         whole = jnp.concatenate(outs, axis=0).astype(BF16)
         back1[...] = whole.reshape(clusters, 2 * MESSAGE, head_dim)
 
+        for dy, dz in away:
+            to_home(ys[dy] * n + zs[dz])
+
         @pl.when(even)
         def _():
-            loop(0, clusters - 1, lambda i: to_home(i, 0))
             home[0, chip // 2] = back1[chip]
 
         @pl.when(jnp.logical_not(even))
         def _():
-            loop(0, clusters, lambda i: to_home(i, 1))
+            to_home(chip)
 
     def back_sent():
         @pl.when((core == 0) & even)
@@ -423,9 +407,11 @@
     swap = copy_to(home.at[core], home.at[core], h_send.at[0], h_recv.at[0], (other, mp))
     swap.start()
     sent.append(swap.wait_send)
+    first_half = dot(unpick[core], home[core].reshape(rows, head_dim))
     take(home.at[0], h_recv.at[0])
 
-    ordered = dot(unpick[...], home[...].reshape(home_rows, head_dim)).astype(BF16)
+    second_half = dot(unpick[1 - core], home[1 - core].reshape(rows, head_dim))
+    ordered = (first_half + second_half).astype(BF16)
     for of in range(2):
         for kind in range(3):
             at = (of * 3 + kind) * tokens
@@ -461,44 +447,45 @@
             part_send.at[to], part_land.at[source], p_send.at[off], p_recv.at[off], device(to, b)
         )
 
-    def send_part(i):
-        off = lax.rem(i + n // 2 - 1, n - 1) + 1
-        to = lax.rem(a + off, n)
-        part_send[to] = partial(to).astype(BF16)
-        part_copy(off, to, a).start()
-
-    loop(0, n - 1, send_part)
-    sent.append(lambda: loop(1, n, lambda i: part_copy(i, lax.rem(a + i, n), a).wait_send()))
+    by_distance = sorted(range(1, n), key=lambda d: -min(d, n - d))
+    for d in by_distance:
+        part_send[firsts[d]] = partial(firsts[d]).astype(BF16)
+        part_copy(d, firsts[d], a).start()
     part_sum[...] = partial(a).reshape(part_sum.shape)
 
-    def add_part(i):
-        source = lax.rem(a + n - i, n)
-        part_copy(i, a, source).wait_recv()
+    def all_sent():
+        for wait_sent in sent:
+            wait_sent()
+        sent.clear()
+
+    all_sent()
+    for d in reversed(by_distance):
+        source = firsts[n - d]
+        part_copy(d, a, source).wait_recv()
         part_sum[...] += part_land[source].astype(F32).reshape(part_sum.shape)
-
-    loop(1, n, add_part)
 
     def last_copy(off, to, source):
         return copy_to(
-            part_sum.at[to], last_land.at[source], l_send.at[off], l_recv.at[off], device(a, to)
+            last_send.at[to], last_land.at[source], l_send.at[off], l_recv.at[off], device(a, to)
         )
 
-    loop(1, n, lambda i: last_copy(i, lax.rem(b + i, n), b).start())
-    sent.append(lambda: loop(1, n, lambda i: last_copy(i, lax.rem(b + i, n), b).wait_send()))
+    last_send[...] = part_sum[...].astype(BF16)
+    for d in by_distance:
+        last_copy(d, seconds[d], b).start()
+        sent.append(last_copy(d, seconds[d], b).wait_send)
     wg_ref[...] = part_sum[b]
-
-    def add_last(i):
-        source = lax.rem(b + n - i, n)
-        last_copy(i, b, source).wait_recv()
-        wg_ref[...] += last_land[source]
-
-    loop(1, n, add_last)
+    for d in by_distance:
+        part_copy(d, firsts[d], a).wait_send()
+
+    for d in reversed(by_distance):
+        source = seconds[n - d]
+        last_copy(d, b, source).wait_recv()
+        wg_ref[...] += last_land[source].astype(F32)
     wg_copy = pltpu.make_async_copy(wg_ref, wg_out, out_sem.at[3])
     wg_copy.start()
     sent.append(wg_copy.wait)
 
-    for wait_sent in sent:
-        wait_sent()
+    all_sent()
 
 
 def hand_out(grads_in, wg_in, dq_out, dk_out, dv_out, wg_out):
@@ -538,7 +525,7 @@
             pltpu.SemaphoreType.REGULAR,
             pltpu.VMEM((heads - 1, tokens, cols), BF16),
             pltpu.VMEM((rows, tokens), BF16),
-            pltpu.VMEM((6 * tokens, 2 * rows), BF16),
+            pltpu.VMEM((2, 6 * tokens, rows), BF16),
             pltpu.VMEM((rows, head_dim), F32),
             pltpu.VMEM((clusters, MESSAGE, head_dim), BF16),
             pltpu.VMEM((2 * clusters, MESSAGE, head_dim), BF16),
@@ -551,7 +538,8 @@
             pltpu.VMEM((n, half, width), BF16),
             pltpu.VMEM((n, half, width), BF16),
             pltpu.VMEM((n, FEATS, width), F32),
-            pltpu.VMEM((n, FEATS, width), F32),
+            pltpu.VMEM((n, FEATS, width), BF16),
+            pltpu.VMEM((n, FEATS, width), BF16),
             pltpu.VMEM((FEATS, width), F32),
             dma((1,)),
             dma((1,)),

time: 63.5 us -> 60.8 us (0.957)
  Pallas kernels: 62.7 us -> 60 us
    pallas_call x1, Pallas kernels: 61.2 us -> 58.4 us  [on_device(): pl.pallas_call(lambda *refs: kernel(n, heads, *refs), out_shape=(jax.Shap...]
where the time goes in v3:
time: 60.8 us; the launch traced here: 60.6 us
  Pallas kernels  60 us (99%)
  between operations  0.64 us (1%)
    pallas_call x1, Pallas kernels, on_device(): pl.pallas_call(lambda *refs: kernel(n, heads, *refs), out_shape=(jax.Shap...  58.4 us
    pallas_call x1, Pallas kernels, on_device(): pl.pallas_call(hand_out, out_shape=(grad_shape, grad_shape, grad_shape, w...  1.54 us

profile of v3, /device:TPU:1, one launch (start us, length us, event | category | flops | bytes accessed | tf_op | source)
XLA Modules:
  0.0 60.6 jit_solution(5824793299484280934)
XLA Ops:
  0.6 58.4 %shard_map.102 = (bf16[3,128,128]{2,1,0:T(8,128)(2,1)}, f32[16,384]{1,0:T(8,128)}) custom-call(bf16[128,512]{1,0:T(8,128)(2,1)} %refs_0_.1, bf16[128,512]{1,0:T(8,128)(2,1)} %refs_1_.1, bf16[128,2048]{1,0:T(8,128)(2,1)} %refs_2_.1, bf16[1,128,128]{2,1,0:T(8,128)(2,1)} %refs_3_.1, bf16[1,128,128]{2,1,0:T(8,128)(2,1)} %refs_4_.1, ...), custom_call_target="tpu_custom_call" | custom-call | tf_op jit(solution)/shard_map/pallas_call | solution.py:512
  59.1 1.5 %shard_map.103 = (bf16[1,128,128]{2,1,0:T(8,128)(2,1)}, bf16[1,128,128]{2,1,0:T(8,128)(2,1)}, bf16[1,128,128]{2,1,0:T(8,128)(2,1)}, f32[16,384]{1,0:T(8,128)}) custom-call(bf16[3,128,128]{2,1,0:T(8,128)(2,1)} %get-tuple-element.6.grads_in, f32[16,384]{1,0:T(8,128)} %get-tuple-element.7.wg_in), custom_call_target="tpu_custom_call" | custom-call | tf_op jit(solution)/shard_map/pallas_call | solution.py:573

commit v4 on v3

--- a/solution.py
+++ b/solution.py
@@ -75,12 +75,13 @@
     qkv_ref,
     cid_ref,
     in_sem,
-    out_sem,
     ready,
     grad_land,
     pick,
     unpick,
     packed,
+    split_ref,
+    join_ref,
     send1,
     land2,
     back1,
@@ -88,13 +89,12 @@
     piece0,
     piece1,
     turned,
-    low_grads,
+    both_ref,
     part_send,
     part_land,
     part_sum,
     last_send,
     last_land,
-    wg_ref,
     c_send,
     c_recv,
     x_send,
@@ -220,7 +220,7 @@
 
     fetches[1].wait()
     head_grad = dot(grad_ref[...], w_part(mp), NT)
-    for off in range(1, heads):
+    for off in sorted(range(1, heads), key=lambda d: min(d, heads - d)):
         grad_copy(off).wait_recv()
         head_grad += dot(grad_land[off - 1], w_part(lax.rem(mp + heads - off, heads)), NT)
     filled = packed[...] + dot(pick[...], head_grad.astype(BF16))
@@ -316,14 +316,24 @@
     def _():
         turned[1, :, pl.ds(mp * blocks, blocks)] = piece1[...]
 
-    @pl.when(core == 0)
-    def _():
-        take(land2.at[pl.ds(0, 2 * clusters - 1)], s_recv.at[0])
-
     count = 2 * clusters * MOST
     lot = min(256, 2 * rows)
     part = lot // KINDS
     lots = 2 * rows // lot
+    out_row = iota((lot, lot), 0)
+    in_row = iota((lot, lot), 1)
+    out_at = out_row % part
+    wanted = (out_at // 2) * MESSAGE + (out_row // part) * 2 + out_at % 2
+    split_ref[...] = as_bf16(wanted == in_row)
+    out_row = iota((lot, 3 * part), 0)
+    in_row = iota((lot, 3 * part), 1)
+    wanted = (out_row // 2 % 4) * part + (out_row // MESSAGE) * 2 + out_row % 2
+    join_ref[...] = as_bf16(wanted == in_row)
+
+    @pl.when(core == 0)
+    def _():
+        take(land2.at[pl.ds(0, 2 * clusters - 1)], s_recv.at[0])
+
 
     odd = lax.rem(chip, 2)
     even = odd == 0
@@ -339,23 +349,14 @@
 
     @pl.when(core == 0)
     def _():
-        out_row = iota((lot, lot), 0)
-        in_row = iota((lot, lot), 1)
-        out_at = out_row % part
-        wanted = (out_at // 2) * MESSAGE + (out_row // part) * 2 + out_at % 2
-        split = as_bf16(wanted == in_row)
-        out_row = iota((lot, 3 * part), 0)
-        in_row = iota((lot, 3 * part), 1)
-        wanted = (out_row // 2 % 4) * part + (out_row // MESSAGE) * 2 + out_row % 2
-        join = as_bf16(wanted == in_row)
-        allowed = iota((count, count), 0) <= iota((count, count), 1)
         got = land2[...].astype(F32).reshape(2 * rows, head_dim).astype(BF16)
         pieces = [[] for _ in range(KINDS)]
         for i in range(lots):
-            parted = dot(split, got[i * lot : (i + 1) * lot]).astype(BF16)
+            parted = dot(split_ref[...], got[i * lot : (i + 1) * lot]).astype(BF16)
             for kind in range(KINDS):
                 pieces[kind].append(parted[kind * part : (kind + 1) * part])
         queries, keys, values, grads = (jnp.concatenate(p, axis=0) for p in pieces)
+        allowed = iota((count, count), 0) <= iota((count, count), 1)
         scores = jnp.where(allowed, dot(keys, queries, NT) * scale, -1e30)
         weights = jnp.exp(scores - jnp.max(scores, axis=0, keepdims=True))
         probs = weights / jnp.sum(weights, axis=0, keepdims=True)
@@ -370,7 +371,7 @@
         for i in range(lots):
             span = slice(i * part, (i + 1) * part)
             three = jnp.concatenate([query_part[span], key_part[span], value_part[span]], axis=0)
-            outs.append(dot(join, three))
+            outs.append(dot(join_ref[...], three))
         whole = jnp.concatenate(outs, axis=0).astype(BF16)
         back1[...] = whole.reshape(clusters, 2 * MESSAGE, head_dim)
 
@@ -412,21 +413,6 @@
 
     second_half = dot(unpick[1 - core], home[1 - core].reshape(rows, head_dim))
     ordered = (first_half + second_half).astype(BF16)
-    for of in range(2):
-        for kind in range(3):
-            at = (of * 3 + kind) * tokens
-            low_grads[of, :, kind * head_dim : (kind + 1) * head_dim] = ordered[at : at + tokens]
-    out_copies = [
-        pltpu.make_async_copy(
-            low_grads.at[core, :, pl.ds(kind * head_dim, head_dim)],
-            grads_out.at[kind],
-            out_sem.at[kind],
-        )
-        for kind in range(3)
-    ]
-    for out_copy in out_copies:
-        out_copy.start()
-        sent.append(out_copy.wait)
     for mine in range(2):
 
         @pl.when(core == mine)
@@ -436,7 +422,15 @@
                     if off or of != mine:
                         input_copy(off, of, mine, True).wait_recv()
 
-    both = jnp.concatenate([low_grads[0], low_grads[1]], axis=0)
+    halves = [
+        jnp.concatenate(
+            [ordered[at : at + tokens] for at in range(of * 3 * tokens, (of + 1) * 3 * tokens, tokens)],
+            axis=1,
+        )
+        for of in range(2)
+    ]
+    both_ref[...] = jnp.concatenate(halves, axis=0)
+    both = both_ref[...]
 
     def partial(to):
         left = [turned[of, to].reshape(half, tokens) for of in range(2)]
@@ -453,6 +447,10 @@
         part_copy(d, firsts[d], a).start()
     part_sum[...] = partial(a).reshape(part_sum.shape)
 
+    for kind in range(3):
+        span = slice(kind * head_dim, (kind + 1) * head_dim)
+        grads_out[kind] = both_ref[pl.ds(pl.multiple_of(core * tokens, tokens), tokens), span]
+
     def all_sent():
         for wait_sent in sent:
             wait_sent()
@@ -473,25 +471,28 @@
     for d in by_distance:
         last_copy(d, seconds[d], b).start()
         sent.append(last_copy(d, seconds[d], b).wait_send)
-    wg_ref[...] = part_sum[b]
+    wg_out[...] = part_sum[b]
     for d in by_distance:
         part_copy(d, firsts[d], a).wait_send()
 
     for d in reversed(by_distance):
         source = seconds[n - d]
         last_copy(d, b, source).wait_recv()
-        wg_ref[...] += last_land[source].astype(F32)
-    wg_copy = pltpu.make_async_copy(wg_ref, wg_out, out_sem.at[3])
-    wg_copy.start()
-    sent.append(wg_copy.wait)
+        wg_out[...] += last_land[source].astype(F32)
 
     all_sent()
 
 
-def hand_out(grads_in, wg_in, dq_out, dk_out, dv_out, wg_out):
-    for kind, out in enumerate((dq_out, dk_out, dv_out)):
-        out[0] = grads_in[kind]
-    wg_out[...] = wg_in[...]
+def hand_out(grads_in, wg_in, dq_out, dk_out, dv_out, wg_out, sem):
+    copies = [
+        pltpu.make_async_copy(grads_in.at[pl.ds(kind, 1)], out, sem.at[kind])
+        for kind, out in enumerate((dq_out, dk_out, dv_out))
+    ]
+    copies.append(pltpu.make_async_copy(wg_in, wg_out, sem.at[3]))
+    for copy in copies:
+        copy.start()
+    for copy in copies:
+        copy.wait()
 
 
 def on_device(layer_input, output_grad, w_out, query_heads, key_heads, value_heads, cluster_ids):
@@ -503,17 +504,22 @@
     clusters = n * n
     rows = clusters * MESSAGE
     half = FEATS * n
+    lot = min(256, 2 * rows)
     blocks = cols // (2 * half)
     width = 3 * head_dim
+    vmem = pl.BlockSpec(memory_space=pltpu.VMEM)
     hbm = pl.BlockSpec(memory_space=pltpu.HBM)
     dma = pltpu.SemaphoreType.DMA
     grad_shape = jax.ShapeDtypeStruct((1, tokens, head_dim), BF16)
     wg_shape = jax.ShapeDtypeStruct((FEATS, width), F32)
     grads, weight_grad = pl.pallas_call(
         lambda *refs: kernel(n, heads, *refs),
-        out_shape=(jax.ShapeDtypeStruct((3, tokens, head_dim), BF16), wg_shape),
+        out_shape=(
+            pltpu.VMEM((3, tokens, head_dim), BF16),
+            pltpu.VMEM((FEATS, width), F32),
+        ),
         in_specs=[hbm] * 7,
-        out_specs=(hbm, hbm),
+        out_specs=(vmem, vmem),
         scratch_shapes=[
             pltpu.VMEM((tokens, cols), BF16),
             pltpu.VMEM((tokens, cols), BF16),
@@ -521,12 +527,13 @@
             pltpu.VMEM((3, tokens, head_dim), BF16),
             pltpu.VMEM((2, 1, tokens), jnp.int32),
             dma((7,)),
-            dma((4,)),
             pltpu.SemaphoreType.REGULAR,
             pltpu.VMEM((heads - 1, tokens, cols), BF16),
             pltpu.VMEM((rows, tokens), BF16),
             pltpu.VMEM((2, 6 * tokens, rows), BF16),
             pltpu.VMEM((rows, head_dim), F32),
+            pltpu.VMEM((lot, lot), BF16),
+            pltpu.VMEM((lot, 3 * lot // KINDS), BF16),
             pltpu.VMEM((clusters, MESSAGE, head_dim), BF16),
             pltpu.VMEM((2 * clusters, MESSAGE, head_dim), BF16),
             pltpu.VMEM((clusters, 2 * MESSAGE, head_dim), BF16),
@@ -534,13 +541,12 @@
             pltpu.VMEM((blocks, n, FEATS, tokens), BF16),
             pltpu.VMEM((n, blocks, FEATS, tokens), BF16),
             pltpu.VMEM((2, n, n, FEATS, tokens), BF16),
-            pltpu.VMEM((2, tokens, width), BF16),
+            pltpu.VMEM((2 * tokens, width), BF16),
             pltpu.VMEM((n, half, width), BF16),
             pltpu.VMEM((n, half, width), BF16),
             pltpu.VMEM((n, FEATS, width), F32),
             pltpu.VMEM((n, FEATS, width), BF16),
             pltpu.VMEM((n, FEATS, width), BF16),
-            pltpu.VMEM((FEATS, width), F32),
             dma((1,)),
             dma((1,)),
             dma((heads - 1,)),
@@ -559,23 +565,29 @@
             dma((n,)),
         ],
         compiler_params=pltpu.CompilerParams(
-            collective_id=0, has_side_effects=True, vmem_limit_bytes=64 * 1024 * 1024
+            collective_id=0, has_side_effects=True, vmem_limit_bytes=40 * 1024 * 1024
         ),
     )(
-        output_grad,
-        layer_input,
-        w_out,
-        query_heads,
-        key_heads,
-        value_heads,
-        cluster_ids.reshape(1, tokens),
+        *(
+            pltpu.with_memory_space_constraint(x, pltpu.HBM)
+            for x in (
+                output_grad,
+                layer_input,
+                w_out,
+                query_heads,
+                key_heads,
+                value_heads,
+                cluster_ids.reshape(1, tokens),
+            )
+        )
     )
     return pl.pallas_call(
         hand_out,
         out_shape=(grad_shape, grad_shape, grad_shape, wg_shape),
-        in_specs=[pl.BlockSpec(memory_space=pltpu.VMEM)] * 2,
-        out_specs=(pl.BlockSpec(memory_space=pltpu.VMEM),) * 4,
-        compiler_params=pltpu.CompilerParams(vmem_limit_bytes=64 * 1024 * 1024),
+        in_specs=[vmem] * 2,
+        out_specs=(hbm,) * 4,
+        scratch_shapes=[dma((4,))],
+        compiler_params=pltpu.CompilerParams(vmem_limit_bytes=16 * 1024 * 1024),
     )(grads, weight_grad)
 
 

time: 60.8 us -> 59.1 us (0.972)
  Pallas kernels: 60 us -> 58.4 us
    pallas_call x1, Pallas kernels: 1.54 us -> 0.68 us  [on_device(): pl.pallas_call(hand_out, out_shape=(grad_shape, grad_shape, grad_shape, w...]
    pallas_call x1, Pallas kernels: 58.4 us -> 57.7 us  [on_device(): pl.pallas_call(lambda *refs: kernel(n, heads, *refs), out_shape=(pltpu.VM...]
where the time goes in v4:
time: 59.1 us; the launch traced here: 59 us
  Pallas kernels  58.4 us (99%)
  between operations  0.64 us (1%)
    pallas_call x1, Pallas kernels, on_device(): pl.pallas_call(lambda *refs: kernel(n, heads, *refs), out_shape=(pltpu.VM...  57.7 us

profile of v4, /device:TPU:1, one launch (start us, length us, event | category | flops | bytes accessed | tf_op | source)
XLA Modules:
  0.0 59.0 jit_solution(6007805897769804796)
XLA Ops:
  0.6 57.7 %shard_map.102 = (bf16[3,128,128]{2,1,0:T(8,128)(2,1)S(1)}, f32[16,384]{1,0:T(8,128)S(1)}) custom-call(bf16[128,512]{1,0:T(8,128)(2,1)} %refs_0_.1, bf16[128,512]{1,0:T(8,128)(2,1)} %refs_1_.1, bf16[128,2048]{1,0:T(8,128)(2,1)} %refs_2_.1, bf16[1,128,128]{2,1,0:T(8,128)(2,1)} %refs_3_.1, bf16[1,128,128]{2,1,0:T(8,128)(2,1)} %refs_4_.1, ...), custom_call_target="tpu_custom_call" | custom-call | tf_op jit(solution)/shard_map/pallas_call | solution.py:515
  58.3 0.7 %shard_map.103 = (bf16[1,128,128]{2,1,0:T(8,128)(2,1)}, bf16[1,128,128]{2,1,0:T(8,128)(2,1)}, bf16[1,128,128]{2,1,0:T(8,128)(2,1)}, f32[16,384]{1,0:T(8,128)}) custom-call(bf16[3,128,128]{2,1,0:T(8,128)(2,1)S(1)} %get-tuple-element.6.grads_in, f32[16,384]{1,0:T(8,128)S(1)} %get-tuple-element.7.wg_in), custom_call_target="tpu_custom_call" | custom-call | tf_op jit(solution)/shard_map/pallas_call | solution.py:584

commit v5 on v4

--- a/solution.py
+++ b/solution.py
@@ -86,15 +86,20 @@
     land2,
     back1,
     home,
-    piece0,
-    piece1,
-    turned,
+    piece,
+    turned0,
+    turned1,
     both_ref,
-    part_send,
-    part_land,
-    part_sum,
-    last_send,
-    last_land,
+    part_send0,
+    part_send1,
+    part_land0,
+    part_land1,
+    part_sum0,
+    part_sum1,
+    last_send0,
+    last_send1,
+    last_land0,
+    last_land1,
     c_send,
     c_recv,
     x_send,
@@ -125,18 +130,18 @@
     y = chip // n
     z = lax.rem(chip, n)
     other = seq + 1 - 2 * core
-    a = y + core * (z - y)
-    b = z + core * (y - z)
-
-    def device(first, second):
-        py = first + core * (second - first)
-        pz = second + core * (first - second)
-        return ((py * n + pz) * 2 + core, mp)
+    row = lax.rem(y, 2)
+    mine = row * 2 + core
+
+    def in_pair(rows_on, cores_on):
+        there = y + rows_on * (1 - 2 * row)
+        return (there * n + z) * 2 + core + cores_on * (1 - 2 * core)
+
+    pair = [(0, 1), (1, 0), (1, 1)]
 
     ys = [lax.rem(y + d, n) for d in range(n)]
     zs = [lax.rem(z + d, n) for d in range(n)]
-    firsts = [ys[d] + core * (zs[d] - ys[d]) for d in range(n)]
-    seconds = [zs[d] + core * (ys[d] - zs[d]) for d in range(n)]
+    pair_rows = [y // 2 for y in ys]
     away = sorted(
         ((dy, dz) for dy in range(n) for dz in range(n) if dy or dz),
         key=lambda d: -min(d[0], n - d[0]) - min(d[1], n - d[1]),
@@ -151,8 +156,10 @@
 
     for off in range(1, heads):
         greet((seq, lax.rem(mp + off, heads)))
-        greet((other, lax.rem(mp + off, heads)))
+        for on in pair:
+            greet((in_pair(*on), lax.rem(mp + off, heads)))
     greet((other, mp))
+    greet((in_pair(1, 1), mp))
     for d in range(1, n):
         greet(((ys[d] * n + z) * 2 + core, mp))
         greet(((y * n + zs[d]) * 2 + core, mp))
@@ -163,7 +170,7 @@
             (
                 (grad_hbm, grad_ref),
                 (w_hbm, w_ref),
-                (cid_hbm, cid_ref.at[core]),
+                (cid_hbm, cid_ref.at[mine]),
                 (q_hbm, qkv_ref.at[pl.ds(0, 1)]),
                 (k_hbm, qkv_ref.at[pl.ds(1, 1)]),
                 (v_hbm, qkv_ref.at[pl.ds(2, 1)]),
@@ -173,7 +180,7 @@
     ]
     for fetch in fetches:
         fetch.start()
-    pl.semaphore_wait(barrier, 3 * (n - 1) + 1 + 2 * (heads - 1))
+    pl.semaphore_wait(barrier, 3 * (n - 1) + 2 + 4 * (heads - 1))
 
     def grad_copy(off):
         return copy_to(
@@ -193,13 +200,17 @@
             ready, inc=1, device_id=((ys[d] * n + z) * 2 + core, mp), device_id_type=MESH
         )
     fetches[2].wait()
-    cid_copy = copy_to(
-        cid_ref.at[core], cid_ref.at[core], c_send.at[0], c_recv.at[0], (other, mp)
-    )
-    cid_copy.start()
-    sent.append(cid_copy.wait_send)
-
-    cid_row = cid_ref[core]
+
+    def cid_copy(i, of):
+        return copy_to(
+            cid_ref.at[of], cid_ref.at[of], c_send.at[i], c_recv.at[i], (in_pair(*pair[i]), mp)
+        )
+
+    for i in range(3):
+        cid_copy(i, mine).start()
+        sent.append(cid_copy(i, mine).wait_send)
+
+    cid_row = cid_ref[mine]
     slot_row = slots(cid_row)[0]
     target_row = cid_row * MOST + slot_row
     r_col = iota((rows, 1), 0)
@@ -265,56 +276,60 @@
     blocks = cols // wide
     for i in range(blocks):
         done = dot(order, input_ref[:, i * wide : (i + 1) * wide], NT).astype(BF16)
-        piece0[i] = done[0:half].reshape(n, FEATS, tokens)
-        piece1[:, i] = done[half:].reshape(n, FEATS, tokens)
-
-    take(cid_ref.at[0], c_recv.at[0])
-    r_row = iota((1, rows), 1)
-    key_row = (r_row // (2 * MESSAGE) * 4 + r_row // MESSAGE % 2) * MOST + r_row % MOST
+        piece[i] = done.reshape(2, n, FEATS, tokens)
+
+    for i, (rows_on, cores_on) in enumerate(pair):
+        cid_copy(
+            i, (row + rows_on * (1 - 2 * row)) * 2 + core + cores_on * (1 - 2 * core)
+        ).wait_recv()
+    home_rows = clusters // 2 * MESSAGE
+    r_row = iota((1, home_rows), 1)
+    key_row = r_row // MESSAGE * 2 * MOST + r_row % MOST
     kind_row = r_row // MOST % KINDS
-    for of in range(2):
+    for of in range(4):
         _, cid_col, slot_col = slots(cid_ref[of])
-        wanted = (cid_col * 2 + of) * MOST + slot_col
+        wanted = cid_col * MOST + slot_col
         for kind in range(3):
-            at = (of * 3 + kind) * tokens
-            for odd in range(2):
-                unpick[odd, at : at + tokens] = as_bf16(
-                    jnp.where(kind_row == kind, key_row + 2 * MOST * odd, -1) == wanted
+            for which in range(2):
+                unpick[which, of, kind * tokens : (kind + 1) * tokens] = as_bf16(
+                    jnp.where(kind_row == kind, key_row + MOST * which, -1) == wanted
                 )
 
-    def input_copy(off, of, to, received=False):
-        at = pl.ds(lax.rem(mp + heads - off, heads) * blocks, blocks)
-        here = pl.ds(mp * blocks, blocks)
-        src, mine, theirs = (
-            (piece0, turned.at[of, here], turned.at[of, at])
-            if to == 0
-            else (piece1, turned.at[of, :, here], turned.at[of, :, at])
+    def input_copy(off, to, received_of=None):
+        at = (
+            lax.rem(mp + heads - off, heads) if received_of is not None else mp
         )
-        sems = (i_send.at[2 * off + to], i_recv.at[2 * off + of])
-        goal = (seq - core + to, lax.rem(mp + off, heads))
-        return copy_to(src, theirs if received else mine, *sems, goal)
+        of = mine if received_of is None else received_of
+        dst = turned0.at[of, at] if to % 2 == 0 else turned1.at[of, :, at]
+        return copy_to(
+            piece.at[to // 2, to % 2],
+            dst,
+            i_send.at[4 * off + to],
+            i_recv.at[4 * off + of],
+            ((((y // 2) * 2 + to // 2) * n + z) * 2 + to % 2, lax.rem(mp + off, heads)),
+        )
 
     def inputs(act):
         for off in range(heads):
-            for to in range(2):
+            for to in range(4):
                 if off == 0:
 
-                    @pl.when(core != to)
+                    @pl.when(mine != to)
                     def _():
                         act(off, to)
                 else:
                     act(off, to)
 
-    inputs(lambda off, to: input_copy(off, core, to).start())
-    sent.append(lambda: inputs(lambda off, to: input_copy(off, core, to).wait_send()))
+    inputs(lambda off, to: input_copy(off, to).start())
+    sent.append(lambda: inputs(lambda off, to: input_copy(off, to).wait_send()))
 
     @pl.when(core == 0)
     def _():
-        turned[0, pl.ds(mp * blocks, blocks)] = piece0[...]
+        turned0[mine, mp] = piece[row, 0]
 
     @pl.when(core == 1)
     def _():
-        turned[1, :, pl.ds(mp * blocks, blocks)] = piece1[...]
+        turned1[mine, :, mp] = piece[row, 1]
 
     count = 2 * clusters * MOST
     lot = min(256, 2 * rows)
@@ -338,13 +353,16 @@
     odd = lax.rem(chip, 2)
     even = odd == 0
 
-    def to_home(to):
+    lot_home = clusters // 2
+    spot = odd * lot_home + chip // 2
+
+    def to_home(to_pair, to_y, to_z):
         copy_to(
-            back1.at[to],
-            home.at[odd, chip // 2],
+            back1.at[to_pair, to_z],
+            home.at[spot],
             b_send.at[0],
             b_recv.at[0],
-            (to * 2 + odd, mp),
+            ((to_y * n + to_z) * 2 + odd, mp),
         ).start()
 
     @pl.when(core == 0)
@@ -372,115 +390,164 @@
             span = slice(i * part, (i + 1) * part)
             three = jnp.concatenate([query_part[span], key_part[span], value_part[span]], axis=0)
             outs.append(dot(join_ref[...], three))
-        whole = jnp.concatenate(outs, axis=0).astype(BF16)
-        back1[...] = whole.reshape(clusters, 2 * MESSAGE, head_dim)
+        whole = jnp.concatenate(outs, axis=0)
+        whole = whole.reshape(n // 2, 2, n, 2, MESSAGE, head_dim).astype(BF16)
+        for i in range(2):
+            back1[:, :, i] = whole[:, i]
 
         for dy, dz in away:
-            to_home(ys[dy] * n + zs[dz])
+            to_home(pair_rows[dy], ys[dy], zs[dz])
 
         @pl.when(even)
         def _():
-            home[0, chip // 2] = back1[chip]
+            home[spot] = back1[y // 2, z]
 
         @pl.when(jnp.logical_not(even))
         def _():
-            to_home(chip)
+            to_home(y // 2, y, z)
 
     def back_sent():
         @pl.when((core == 0) & even)
         def _():
-            take(back1.at[pl.ds(0, clusters - 1)], b_send.at[0])
+            take(home.at[pl.ds(0, clusters - 1)], b_send.at[0])
 
         @pl.when((core == 0) & jnp.logical_not(even))
         def _():
-            take(back1, b_send.at[0])
+            take(home, b_send.at[0])
 
     sent.append(back_sent)
 
     @pl.when((core == 0) & even)
     def _():
-        take(home.at[0, pl.ds(0, clusters // 2 - 1)], b_recv.at[0])
+        take(home.at[pl.ds(0, lot_home - 1)], b_recv.at[0])
 
     @pl.when((core == 1) | jnp.logical_not(even))
     def _():
-        take(home.at[0], b_recv.at[0])
-
-    swap = copy_to(home.at[core], home.at[core], h_send.at[0], h_recv.at[0], (other, mp))
+        take(home.at[pl.ds(0, lot_home)], b_recv.at[0])
+
+    own_half = pl.ds(core * lot_home, lot_home)
+    other_half = pl.ds((1 - core) * lot_home, lot_home)
+    swap = copy_to(home.at[own_half], home.at[own_half], h_send.at[0], h_recv.at[0], (other, mp))
     swap.start()
     sent.append(swap.wait_send)
-    first_half = dot(unpick[core], home[core].reshape(rows, head_dim))
-    take(home.at[0], h_recv.at[0])
-
-    second_half = dot(unpick[1 - core], home[1 - core].reshape(rows, head_dim))
-    ordered = (first_half + second_half).astype(BF16)
-    for mine in range(2):
-
-        @pl.when(core == mine)
+
+    def order_half(which, span, of):
+        got = home[span, of // 2, of % 2].astype(F32).reshape(home_rows, head_dim).astype(BF16)
+        return dot(unpick[which, of], got)
+
+    first_half = [order_half(core, own_half, of) for of in range(4)]
+    take(home.at[pl.ds(0, lot_home)], h_recv.at[0])
+
+    for of in range(4):
+        ordered = (first_half[of] + order_half(1 - core, other_half, of)).astype(BF16)
+        for kind in range(3):
+            both_ref[
+                of * tokens : (of + 1) * tokens, kind * head_dim : (kind + 1) * head_dim
+            ] = ordered[kind * tokens : (kind + 1) * tokens]
+    for which in range(2):
+
+        @pl.when(core == which)
         def _():
             for off in range(heads):
-                for of in range(2):
-                    if off or of != mine:
-                        input_copy(off, of, mine, True).wait_recv()
-
-    halves = [
-        jnp.concatenate(
-            [ordered[at : at + tokens] for at in range(of * 3 * tokens, (of + 1) * 3 * tokens, tokens)],
-            axis=1,
-        )
-        for of in range(2)
-    ]
-    both_ref[...] = jnp.concatenate(halves, axis=0)
-    both = both_ref[...]
-
-    def partial(to):
-        left = [turned[of, to].reshape(half, tokens) for of in range(2)]
-        return dot(jnp.concatenate(left, axis=1), both)
-
-    def part_copy(off, to, source):
-        return copy_to(
-            part_send.at[to], part_land.at[source], p_send.at[off], p_recv.at[off], device(to, b)
-        )
-
-    by_distance = sorted(range(1, n), key=lambda d: -min(d, n - d))
-    for d in by_distance:
-        part_send[firsts[d]] = partial(firsts[d]).astype(BF16)
-        part_copy(d, firsts[d], a).start()
-    part_sum[...] = partial(a).reshape(part_sum.shape)
+                for of in range(4):
+                    if off or of % 2 != which:
+                        input_copy(off, which, of).wait_recv()
+                    else:
+
+                        @pl.when(row != of // 2)
+                        def _():
+                            input_copy(off, which, of).wait_recv()
+
+    class Sums:
+        def __init__(self, which):
+            in_y = (n // 2, pair_rows, lambda i: ((i * 2 + row) * n + z) * 2 + which)
+            in_z = (n, zs, lambda i: (y * n + i) * 2 + which)
+            self.first, self.second = (in_y, in_z) if which == 0 else (in_z, in_y)
+            self.turned = (turned0, turned1)[which]
+            self.part_send = (part_send0, part_send1)[which]
+            self.part_land = (part_land0, part_land1)[which]
+            self.part_sum = (part_sum0, part_sum1)[which]
+            self.last_send = (last_send0, last_send1)[which]
+            self.last_land = (last_land0, last_land1)[which]
+
+        @staticmethod
+        def places(axis):
+            size, near, _ = axis
+            steps = [rem_at(near, size, d) for d in range(size)]
+            far = sorted(range(1, size), key=lambda d: -min(d, size - d))
+            return [(d, steps[d], steps[size - d]) for d in far], steps[0]
+
+        def part_copy(self, d, to, source):
+            return copy_to(
+                self.part_send.at[to],
+                self.part_land.at[source],
+                p_send.at[d],
+                p_recv.at[d],
+                (self.first[2](to), mp),
+            )
+
+        def last_copy(self, d, to, source):
+            return copy_to(
+                self.last_send.at[to],
+                self.last_land.at[source],
+                l_send.at[d],
+                l_recv.at[d],
+                (self.second[2](to), mp),
+            )
+
+        def partial(self, to, both):
+            high = self.part_send.shape[1]
+            left = [self.turned[of, to].reshape(high, tokens) for of in range(4)]
+            return dot(jnp.concatenate(left, axis=1), both)
+
+        def begin(self):
+            both = both_ref[...]
+            others, here = self.places(self.first)
+            for d, to, _ in others:
+                self.part_send[to] = self.partial(to, both).astype(BF16)
+                self.part_copy(d, to, here).start()
+            self.part_sum[...] = self.partial(here, both).reshape(self.part_sum.shape)
+
+        def finish(self):
+            others, here = self.places(self.first)
+            for d, _, source in reversed(others):
+                self.part_copy(d, here, source).wait_recv()
+                self.part_sum[...] += (
+                    self.part_land[source].astype(F32).reshape(self.part_sum.shape)
+                )
+            self.last_send[...] = self.part_sum[...].astype(BF16)
+            lasts, last_here = self.places(self.second)
+            for d, to, _ in lasts:
+                self.last_copy(d, to, last_here).start()
+            wg_out[...] = self.part_sum[last_here]
+            for d, to, _ in others:
+                self.part_copy(d, to, here).wait_send()
+            for d, _, source in reversed(lasts):
+                self.last_copy(d, last_here, source).wait_recv()
+                wg_out[...] += self.last_land[source].astype(F32)
+            for d, to, _ in lasts:
+                self.last_copy(d, to, last_here).wait_send()
+
+    def rem_at(near, size, d):
+        return near[d] if size == n else near[2 * d]
+
+    for which in range(2):
+
+        @pl.when(core == which)
+        def _():
+            Sums(which).begin()
 
     for kind in range(3):
         span = slice(kind * head_dim, (kind + 1) * head_dim)
-        grads_out[kind] = both_ref[pl.ds(pl.multiple_of(core * tokens, tokens), tokens), span]
-
-    def all_sent():
-        for wait_sent in sent:
-            wait_sent()
-        sent.clear()
-
-    all_sent()
-    for d in reversed(by_distance):
-        source = firsts[n - d]
-        part_copy(d, a, source).wait_recv()
-        part_sum[...] += part_land[source].astype(F32).reshape(part_sum.shape)
-
-    def last_copy(off, to, source):
-        return copy_to(
-            last_send.at[to], last_land.at[source], l_send.at[off], l_recv.at[off], device(a, to)
-        )
-
-    last_send[...] = part_sum[...].astype(BF16)
-    for d in by_distance:
-        last_copy(d, seconds[d], b).start()
-        sent.append(last_copy(d, seconds[d], b).wait_send)
-    wg_out[...] = part_sum[b]
-    for d in by_distance:
-        part_copy(d, firsts[d], a).wait_send()
-
-    for d in reversed(by_distance):
-        source = seconds[n - d]
-        last_copy(d, b, source).wait_recv()
-        wg_out[...] += last_land[source].astype(F32)
-
-    all_sent()
+        grads_out[kind] = both_ref[pl.ds(pl.multiple_of(mine * tokens, tokens), tokens), span]
+    for wait_sent in sent:
+        wait_sent()
+
+    for which in range(2):
+
+        @pl.when(core == which)
+        def _():
+            Sums(which).finish()
 
 
 def hand_out(grads_in, wg_in, dq_out, dk_out, dv_out, wg_out, sem):
@@ -505,7 +572,6 @@
     rows = clusters * MESSAGE
     half = FEATS * n
     lot = min(256, 2 * rows)
-    blocks = cols // (2 * half)
     width = 3 * head_dim
     vmem = pl.BlockSpec(memory_space=pltpu.VMEM)
     hbm = pl.BlockSpec(memory_space=pltpu.HBM)
@@ -525,34 +591,39 @@
             pltpu.VMEM((tokens, cols), BF16),
             pltpu.VMEM((head_dim, heads * cols), BF16),
             pltpu.VMEM((3, tokens, head_dim), BF16),
-            pltpu.VMEM((2, 1, tokens), jnp.int32),
+            pltpu.VMEM((4, 1, tokens), jnp.int32),
             dma((7,)),
             pltpu.SemaphoreType.REGULAR,
             pltpu.VMEM((heads - 1, tokens, cols), BF16),
             pltpu.VMEM((rows, tokens), BF16),
-            pltpu.VMEM((2, 6 * tokens, rows), BF16),
+            pltpu.VMEM((2, 4, 3 * tokens, rows // 2), BF16),
             pltpu.VMEM((rows, head_dim), F32),
             pltpu.VMEM((lot, lot), BF16),
             pltpu.VMEM((lot, 3 * lot // KINDS), BF16),
             pltpu.VMEM((clusters, MESSAGE, head_dim), BF16),
             pltpu.VMEM((2 * clusters, MESSAGE, head_dim), BF16),
-            pltpu.VMEM((clusters, 2 * MESSAGE, head_dim), BF16),
-            pltpu.VMEM((2, clusters // 2, 2 * MESSAGE, head_dim), BF16),
-            pltpu.VMEM((blocks, n, FEATS, tokens), BF16),
-            pltpu.VMEM((n, blocks, FEATS, tokens), BF16),
-            pltpu.VMEM((2, n, n, FEATS, tokens), BF16),
-            pltpu.VMEM((2 * tokens, width), BF16),
-            pltpu.VMEM((n, half, width), BF16),
-            pltpu.VMEM((n, half, width), BF16),
+            pltpu.VMEM((n // 2, n, 2, 2, MESSAGE, head_dim), BF16),
+            pltpu.VMEM((clusters, 2, 2, MESSAGE, head_dim), BF16),
+            pltpu.VMEM((2, 2, n, FEATS, tokens), BF16),
+            pltpu.VMEM((4, n // 2, n, FEATS, tokens), BF16),
+            pltpu.VMEM((4, n, n // 2, FEATS, tokens), BF16),
+            pltpu.VMEM((4 * tokens, width), BF16),
+            pltpu.VMEM((n // 2, half, width), BF16),
+            pltpu.VMEM((n, half // 2, width), BF16),
+            pltpu.VMEM((n // 2, half, width), BF16),
+            pltpu.VMEM((n, half // 2, width), BF16),
             pltpu.VMEM((n, FEATS, width), F32),
+            pltpu.VMEM((n // 2, FEATS, width), F32),
             pltpu.VMEM((n, FEATS, width), BF16),
+            pltpu.VMEM((n // 2, FEATS, width), BF16),
             pltpu.VMEM((n, FEATS, width), BF16),
-            dma((1,)),
-            dma((1,)),
+            pltpu.VMEM((n // 2, FEATS, width), BF16),
+            dma((3,)),
+            dma((3,)),
             dma((heads - 1,)),
             dma((heads - 1,)),
-            dma((2 * heads,)),
-            dma((2 * heads,)),
+            dma((4 * heads,)),
+            dma((4 * heads,)),
             dma((1,)),
             dma((1,)),
             dma((1,)),

time: 59.1 us -> 57.8 us (0.978)
  Pallas kernels: 58.4 us -> 57.1 us
    pallas_call x1, Pallas kernels: 57.7 us -> 56.4 us  [on_device(): pl.pallas_call(lambda *refs: kernel(n, heads, *refs), out_shape=(pltpu.VM...]
where the time goes in v5:
time: 57.8 us; the launch traced here: 57.7 us
  Pallas kernels  57.1 us (99%)
  between operations  0.64 us (1%)
    pallas_call x1, Pallas kernels, on_device(): pl.pallas_call(lambda *refs: kernel(n, heads, *refs), out_shape=(pltpu.VM...  56.4 us

profile of v5, /device:TPU:1, one launch (start us, length us, event | category | flops | bytes accessed | tf_op | source)
XLA Modules:
  0.0 57.7 jit_solution(14684011702181574082)
XLA Ops:
  0.6 56.4 %shard_map.102 = (bf16[3,128,128]{2,1,0:T(8,128)(2,1)S(1)}, f32[16,384]{1,0:T(8,128)S(1)}) custom-call(bf16[128,512]{1,0:T(8,128)(2,1)} %refs_0_.1, bf16[128,512]{1,0:T(8,128)(2,1)} %refs_1_.1, bf16[128,2048]{1,0:T(8,128)(2,1)} %refs_2_.1, bf16[1,128,128]{2,1,0:T(8,128)(2,1)} %refs_3_.1, bf16[1,128,128]{2,1,0:T(8,128)(2,1)} %refs_4_.1, ...), custom_call_target="tpu_custom_call" | custom-call | tf_op jit(solution)/shard_map/pallas_call | solution.py:581
  57.0 0.7 %shard_map.103 = (bf16[1,128,128]{2,1,0:T(8,128)(2,1)}, bf16[1,128,128]{2,1,0:T(8,128)(2,1)}, bf16[1,128,128]{2,1,0:T(8,128)(2,1)}, f32[16,384]{1,0:T(8,128)}) custom-call(bf16[3,128,128]{2,1,0:T(8,128)(2,1)S(1)} %get-tuple-element.6.grads_in, f32[16,384]{1,0:T(8,128)S(1)} %get-tuple-element.7.wg_in), custom_call_target="tpu_custom_call" | custom-call | tf_op jit(solution)/shard_map/pallas_call | solution.py:655

commit v6 on v5

--- a/solution.py
+++ b/solution.py
@@ -81,7 +81,7 @@
     unpick,
     packed,
     split_ref,
-    join_ref,
+    mask_ref,
     send1,
     land2,
     back1,
@@ -282,18 +282,16 @@
         cid_copy(
             i, (row + rows_on * (1 - 2 * row)) * 2 + core + cores_on * (1 - 2 * core)
         ).wait_recv()
-    home_rows = clusters // 2 * MESSAGE
+    home_rows = clusters // 2 * 4 * MOST
     r_row = iota((1, home_rows), 1)
-    key_row = r_row // MESSAGE * 2 * MOST + r_row % MOST
-    kind_row = r_row // MOST % KINDS
+    key_row = r_row // (4 * MOST) * 8 * MOST + r_row % (4 * MOST)
     for of in range(4):
         _, cid_col, slot_col = slots(cid_ref[of])
-        wanted = cid_col * MOST + slot_col
-        for kind in range(3):
-            for which in range(2):
-                unpick[which, of, kind * tokens : (kind + 1) * tokens] = as_bf16(
-                    jnp.where(kind_row == kind, key_row + MOST * which, -1) == wanted
-                )
+        wanted = (cid_col * 4 + of) * MOST + slot_col
+        for which in range(2):
+            unpick[which, of * tokens : (of + 1) * tokens] = as_bf16(
+                key_row + 4 * MOST * which == wanted
+            )
 
     def input_copy(off, to, received_of=None):
         at = (
@@ -337,13 +335,18 @@
     lots = 2 * rows // lot
     out_row = iota((lot, lot), 0)
     in_row = iota((lot, lot), 1)
-    out_at = out_row % part
-    wanted = (out_at // 2) * MESSAGE + (out_row // part) * 2 + out_at % 2
+
+    def source(p):
+        first = p // (4 * MOST * n)
+        second = p // (4 * MOST) % n
+        return ((first * 2 + p // (2 * MOST) % 2) * n + second) * 2 * MOST + p % (2 * MOST)
+
+    token = source(out_row % part)
+    wanted = (token // MOST) * MESSAGE + (out_row // part) * MOST + token % MOST
     split_ref[...] = as_bf16(wanted == in_row)
-    out_row = iota((lot, 3 * part), 0)
-    in_row = iota((lot, 3 * part), 1)
-    wanted = (out_row // 2 % 4) * part + (out_row // MESSAGE) * 2 + out_row % 2
-    join_ref[...] = as_bf16(wanted == in_row)
+    mask_ref[...] = jnp.where(
+        source(iota((count, 1), 0)) <= source(iota((1, count), 1)), 0.0, -1e30
+    )
 
     @pl.when(core == 0)
     def _():
@@ -358,7 +361,7 @@
 
     def to_home(to_pair, to_y, to_z):
         copy_to(
-            back1.at[to_pair, to_z],
+            back1.at[to_pair * n + to_z],
             home.at[spot],
             b_send.at[0],
             b_recv.at[0],
@@ -374,33 +377,27 @@
             for kind in range(KINDS):
                 pieces[kind].append(parted[kind * part : (kind + 1) * part])
         queries, keys, values, grads = (jnp.concatenate(p, axis=0) for p in pieces)
-        allowed = iota((count, count), 0) <= iota((count, count), 1)
-        scores = jnp.where(allowed, dot(keys, queries, NT) * scale, -1e30)
+        scores = jnp.where(mask_ref[...] < 0, -1e30, dot(keys, queries, NT) * scale)
         weights = jnp.exp(scores - jnp.max(scores, axis=0, keepdims=True))
         probs = weights / jnp.sum(weights, axis=0, keepdims=True)
         probs_low = probs.astype(BF16)
         prob_grad = dot(values, grads, NT)
         delta = jnp.sum(probs_low.astype(F32) * prob_grad, axis=0, keepdims=True)
         dscore = (probs * (prob_grad - delta)).astype(BF16)
-        value_part = dot(probs_low, grads).astype(BF16)
-        key_part = (dot(dscore, queries) * scale).astype(BF16)
-        query_part = (dot(dscore, keys, TN) * scale).astype(BF16)
-        outs = []
-        for i in range(lots):
-            span = slice(i * part, (i + 1) * part)
-            three = jnp.concatenate([query_part[span], key_part[span], value_part[span]], axis=0)
-            outs.append(dot(join_ref[...], three))
-        whole = jnp.concatenate(outs, axis=0)
-        whole = whole.reshape(n // 2, 2, n, 2, MESSAGE, head_dim).astype(BF16)
-        for i in range(2):
-            back1[:, :, i] = whole[:, i]
+        parts = (
+            dot(dscore, keys, TN) * scale,
+            dot(dscore, queries) * scale,
+            dot(probs_low, grads),
+        )
+        for kind in range(3):
+            back1[:, kind] = parts[kind].reshape(-1, 4 * MOST, head_dim).astype(BF16)
 
         for dy, dz in away:
             to_home(pair_rows[dy], ys[dy], zs[dz])
 
         @pl.when(even)
         def _():
-            home[spot] = back1[y // 2, z]
+            home[spot] = back1[y // 2 * n + z]
 
         @pl.when(jnp.logical_not(even))
         def _():
@@ -431,19 +428,16 @@
     swap.start()
     sent.append(swap.wait_send)
 
-    def order_half(which, span, of):
-        got = home[span, of // 2, of % 2].astype(F32).reshape(home_rows, head_dim).astype(BF16)
-        return dot(unpick[which, of], got)
-
-    first_half = [order_half(core, own_half, of) for of in range(4)]
+    def order_half(which, span, kind):
+        got = home[span, kind].astype(F32).reshape(home_rows, head_dim).astype(BF16)
+        return dot(unpick[which], got)
+
+    first_half = [order_half(core, own_half, kind) for kind in range(3)]
     take(home.at[pl.ds(0, lot_home)], h_recv.at[0])
 
-    for of in range(4):
-        ordered = (first_half[of] + order_half(1 - core, other_half, of)).astype(BF16)
-        for kind in range(3):
-            both_ref[
-                of * tokens : (of + 1) * tokens, kind * head_dim : (kind + 1) * head_dim
-            ] = ordered[kind * tokens : (kind + 1) * tokens]
+    for kind in range(3):
+        ordered = first_half[kind] + order_half(1 - core, other_half, kind)
+        both_ref[:, kind * head_dim : (kind + 1) * head_dim] = ordered.astype(BF16)
     for which in range(2):
 
         @pl.when(core == which)
@@ -596,14 +590,14 @@
             pltpu.SemaphoreType.REGULAR,
             pltpu.VMEM((heads - 1, tokens, cols), BF16),
             pltpu.VMEM((rows, tokens), BF16),
-            pltpu.VMEM((2, 4, 3 * tokens, rows // 2), BF16),
+            pltpu.VMEM((2, 4 * tokens, rows // 2), BF16),
             pltpu.VMEM((rows, head_dim), F32),
             pltpu.VMEM((lot, lot), BF16),
-            pltpu.VMEM((lot, 3 * lot // KINDS), BF16),
+            pltpu.VMEM((2 * clusters * MOST, 2 * clusters * MOST), F32),
             pltpu.VMEM((clusters, MESSAGE, head_dim), BF16),
             pltpu.VMEM((2 * clusters, MESSAGE, head_dim), BF16),
-            pltpu.VMEM((n // 2, n, 2, 2, MESSAGE, head_dim), BF16),
-            pltpu.VMEM((clusters, 2, 2, MESSAGE, head_dim), BF16),
+            pltpu.VMEM((clusters // 2, 3, 4 * MOST, head_dim), BF16),
+            pltpu.VMEM((clusters, 3, 4 * MOST, head_dim), BF16),
             pltpu.VMEM((2, 2, n, FEATS, tokens), BF16),
             pltpu.VMEM((4, n // 2, n, FEATS, tokens), BF16),
             pltpu.VMEM((4, n, n // 2, FEATS, tokens), BF16),

time: 57.8 us -> 56.1 us (0.971)
  Pallas kernels: 57.1 us -> 55.4 us
    pallas_call x1, Pallas kernels: 56.4 us -> 54.7 us  [on_device(): pl.pallas_call(lambda *refs: kernel(n, heads, *refs), out_shape=(pltpu.VM...]
where the time goes in v6:
time: 56.1 us; the launch traced here: 56 us
  Pallas kernels  55.4 us (99%)
  between operations  0.64 us (1%)
    pallas_call x1, Pallas kernels, on_device(): pl.pallas_call(lambda *refs: kernel(n, heads, *refs), out_shape=(pltpu.VM...  54.7 us

profile of v6, /device:TPU:1, one launch (start us, length us, event | category | flops | bytes accessed | tf_op | source)
XLA Modules:
  0.0 56.0 jit_solution(18189371059708573155)
XLA Ops:
  0.6 54.7 %shard_map.102 = (bf16[3,128,128]{2,1,0:T(8,128)(2,1)S(1)}, f32[16,384]{1,0:T(8,128)S(1)}) custom-call(bf16[128,512]{1,0:T(8,128)(2,1)} %refs_0_.1, bf16[128,512]{1,0:T(8,128)(2,1)} %refs_1_.1, bf16[128,2048]{1,0:T(8,128)(2,1)} %refs_2_.1, bf16[1,128,128]{2,1,0:T(8,128)(2,1)} %refs_3_.1, bf16[1,128,128]{2,1,0:T(8,128)(2,1)} %refs_4_.1, ...), custom_call_target="tpu_custom_call" | custom-call | tf_op jit(solution)/shard_map/pallas_call | solution.py:575
  55.3 0.7 %shard_map.103 = (bf16[1,128,128]{2,1,0:T(8,128)(2,1)}, bf16[1,128,128]{2,1,0:T(8,128)(2,1)}, bf16[1,128,128]{2,1,0:T(8,128)(2,1)}, f32[16,384]{1,0:T(8,128)}) custom-call(bf16[3,128,128]{2,1,0:T(8,128)(2,1)S(1)} %get-tuple-element.6.grads_in, f32[16,384]{1,0:T(8,128)S(1)} %get-tuple-element.7.wg_in), custom_call_target="tpu_custom_call" | custom-call | tf_op jit(solution)/shard_map/pallas_call | solution.py:649

commit v7 on v6

--- a/solution.py
+++ b/solution.py
@@ -192,7 +192,7 @@
         )
 
     fetches[0].wait()
-    for off in range(1, heads):
+    for off in sorted(range(1, heads), key=lambda d: -min(d, heads - d)):
         grad_copy(off).start()
         sent.append(grad_copy(off).wait_send)
     for d in range(1, n):

time: 56.1 us -> 56.2 us (level)
  no operation moved by 1% of the time
where the time goes in v7:
time: 56.2 us; the launch traced here: 56 us
  Pallas kernels  55.4 us (99%)
  between operations  0.64 us (1%)
    pallas_call x1, Pallas kernels, on_device(): pl.pallas_call(lambda *refs: kernel(n, heads, *refs), out_shape=(pltpu.VM...  54.7 us

profile of v7, /device:TPU:1, one launch (start us, length us, event | category | flops | bytes accessed | tf_op | source)
XLA Modules:
  0.0 56.0 jit_solution(417897255846085437)
XLA Ops:
  0.6 54.7 %shard_map.102 = (bf16[3,128,128]{2,1,0:T(8,128)(2,1)S(1)}, f32[16,384]{1,0:T(8,128)S(1)}) custom-call(bf16[128,512]{1,0:T(8,128)(2,1)} %refs_0_.1, bf16[128,512]{1,0:T(8,128)(2,1)} %refs_1_.1, bf16[128,2048]{1,0:T(8,128)(2,1)} %refs_2_.1, bf16[1,128,128]{2,1,0:T(8,128)(2,1)} %refs_3_.1, bf16[1,128,128]{2,1,0:T(8,128)(2,1)} %refs_4_.1, ...), custom_call_target="tpu_custom_call" | custom-call | tf_op jit(solution)/shard_map/pallas_call | solution.py:575
  55.4 0.7 %shard_map.103 = (bf16[1,128,128]{2,1,0:T(8,128)(2,1)}, bf16[1,128,128]{2,1,0:T(8,128)(2,1)}, bf16[1,128,128]{2,1,0:T(8,128)(2,1)}, f32[16,384]{1,0:T(8,128)}) custom-call(bf16[3,128,128]{2,1,0:T(8,128)(2,1)S(1)} %get-tuple-element.6.grads_in, f32[16,384]{1,0:T(8,128)S(1)} %get-tuple-element.7.wg_in), custom_call_target="tpu_custom_call" | custom-call | tf_op jit(solution)/shard_map/pallas_call | solution.py:649
